TPU v7x, 32 devices: a whole 2x2x4 slice. The times are simulated.
32 devices in a mesh: grp: 2 (over y), tm: 8 (over z, x), inp: 2 (over core).
Axes of the slice: x: 2, y: 2, z: 4, core: 2. Of those that a mesh axis runs over, the one named last changes fastest.
Arguments:
- raw_samples: bfloat16 [4096, 16384], P(('grp', 'inp'), 'tm'), parts along dimension 0, may hold values from -24 to 24
- pfb_window: float32 [4, 2048], replicated, may hold values from -0.75 to 0.75
- tile_table: int32 [36, 2], P('inp'), may hold values from 0 to 7, as said below
Outputs:
- visibility: bfloat16 [128, 36, 2, 256, 256], P(('grp', 'tm'), 'inp'), parts along dimension 0
There are 2 independent parts, one for each index of `grp`. A program takes and returns all parts, laid end to end along the dimension named above; an argument that names none is the same for every part. Nothing has to cross between parts.
Inputs may be any that keep to these rules, and one draw needn't show every extreme that they name: `tile_table`: each pair of input blocks (p, q) with p <= q < 8 stands in exactly one row, as [p, q].
All inputs are finite; a program needn't handle non-finite values.
Results may differ from a plain program's by a relative error of at most 0.0057.
Values may be sent and summed in bfloat16 or wider, within the bound.
No kernel may reach another device: no remote copies, remote signals or barrier semaphores. Data moves between devices by JAX's collectives and lax.ppermute only.
A program may use at most 192 MiB of HBM per device.

v0:
```python
import jax
import jax.numpy as jnp
from jax import lax
from jax.sharding import PartitionSpec as P

INPUTS = 2048
NFFT = 2048
TAPS = 4
CHAN = 64
TILE = 256


def shifted(array, axis, by):
    size = lax.axis_size(axis)
    pairs = [(i, i + by) for i in range(size) if 0 <= i + by < size]
    return lax.ppermute(array, axis, pairs)


def channel_basis():
    sample_index = jnp.arange(NFFT, dtype=jnp.int32)
    channel_index = CHAN + jnp.arange(CHAN, dtype=jnp.int32)
    wrapped = sample_index[:, None] * channel_index[None, :] % NFFT
    phase_angle = wrapped.astype(jnp.float32) * (2.0 * jnp.pi / NFFT)
    scale = 1.0 / jnp.sqrt(jnp.float32(NFFT))
    return jnp.concatenate([jnp.cos(phase_angle), -jnp.sin(phase_angle)], axis=1) * scale


def transform(frame_block, cosine_table):
    spectrum = jnp.einsum("fin,nc->fci", frame_block, cosine_table, precision=lax.Precision.HIGHEST)
    return spectrum.reshape(frame_block.shape[0], 2, CHAN, frame_block.shape[1])


def add_leading(running, received):
    sent_frames = received.shape[0]
    return jnp.concatenate([running + received, running[sent_frames:]], axis=0)


def filter_pieces(samples, pfb_window):
    inp_dev, frames, width = samples.shape
    frame = 0
    running = pfb_window[0][None, :] * samples[:, frame, :]
    local_frames = [running]
    filtered = jnp.stack(local_frames)
    max_distance = (TAPS - 2) // frames + 1
    outgoing = []
    for distance in range(1, max_distance + 1):
        frame = 0
        running = jnp.zeros((inp_dev, width), jnp.float32)
        for tap_lag in range(
            frame + (distance - 1) * frames + 1, min(TAPS - 1, frame + distance * frames) + 1
        ):
            source = frame + distance * frames - tap_lag
            running = pfb_window[tap_lag][None, :] * samples[:, source, :]
        partial_list = [running]
        outgoing.append(jnp.stack(partial_list))
    return (filtered, outgoing)


def corner_turn(spectra):
    return lax.all_to_all(
        spectra.astype(jnp.bfloat16), "tm", split_axis=2, concat_axis=0, tiled=True
    )


def local(raw_samples, pfb_window, tile_table):
    inp_dev, sample_count = raw_samples.shape
    frames = sample_count // NFFT
    samples = raw_samples.astype(jnp.float32).reshape(inp_dev, frames, NFFT)
    cosine_table = channel_basis()
    filtered, outgoing = filter_pieces(samples, pfb_window)
    for distance in range(1, len(outgoing) + 1):
        received = shifted(outgoing[distance - 1], "tm", distance)
        filtered = add_leading(filtered, received)
    turned = corner_turn(transform(filtered, cosine_table))
    gathered = lax.all_gather(turned, "inp", axis=3, tiled=True)
    frame_count = gathered.shape[0]
    chan_count = gathered.shape[2]
    blocks = gathered.reshape(frame_count, 2, chan_count, INPUTS // TILE, TILE)
    left_blocks = jnp.take(blocks, tile_table[:, 0], axis=3)
    right_blocks = jnp.take(blocks, tile_table[:, 1], axis=3)
    left_real = left_blocks[:, 0]
    left_imag = left_blocks[:, 1]
    stacked_left = jnp.concatenate([left_real, left_imag], axis=0)
    rotated = jnp.concatenate([left_imag, -left_real], axis=0)
    combined = jnp.concatenate([stacked_left, rotated], axis=3)
    stacked_right = jnp.concatenate([right_blocks[:, 0], right_blocks[:, 1]], axis=0)
    products = jnp.einsum(
        "sctu,sctv->ctuv", combined, stacked_right, preferred_element_type=jnp.float32
    )
    products = products.reshape(chan_count, tile_table.shape[0], 2, TILE, TILE) * (
        1.0 / frame_count
    )
    return products.astype(jnp.bfloat16)


def solution(mesh):
    return jax.shard_map(
        local,
        mesh=mesh,
        in_specs=(P(("grp", "inp"), "tm"), P(), P("inp", None)),
        out_specs=P(("grp", "tm"), "inp", None, None, None),
        check_vma=False,
    )
```

profile of v0, /device:TPU:0, one launch (start us, length us, event | category | flops | bytes accessed | tf_op | source)
XLA Modules:
  0.0 791.5 jit_solution(5774651230545515109)
XLA Ops:
  0.0 0.9 fusion.38
  0.9 12.3 %fusion.7 = (f32[1,1024,2048]{2,1,0:T(8,128)}, f32[1,1024,2048]{2,1,0:T(8,128)}, f32[1,1024,2048]{2,1,0:T(8,128)}) fusion(bf16[1024,2048]{1,0:T(8,128)(2,1)} %param.5, f32[2048]{0:T(1024)S(1)} %bitcast.72, f32[2048]{0:T(1024)S(1)} %bitcast.74, f32[2048]{0:T(1024)S(1)} %bitcast.73), kind=kLoop, calls=%fused_computation.13 | loop fusion | flops 8388608 | bytes 29384704 | tf_op jit(solution)/shard_map/stack | solution.py:55
  13.3 5.4 collective-permute-start
  18.6 6.2 collective-permute-start.1
  24.8 4.5 collective-permute-start.2
  29.3 2.1 fusion.35
  31.4 0.1 maximum_multiply_fusion
  31.5 166.6 %collective-permute-done = f32[1,1024,2048]{2,1,0:T(8,128)S(1)} collective-permute-done((f32[1,1024,2048]{2,1,0:T(8,128)}, f32[1,1024,2048]{2,1,0:T(8,128)S(1)}, u32[]{:S(2)}, u32[]{:S(2)}) %collective-permute-start) | collective-permute-done | bytes 8388640 | tf_op jit(solution)/shard_map/ppermute | solution.py:16
  198.1 4.7 collective-permute-done.1
  202.8 178.3 %collective-permute-done.2 = f32[1,1024,2048]{2,1,0:T(8,128)} collective-permute-done((f32[1,1024,2048]{2,1,0:T(8,128)}, f32[1,1024,2048]{2,1,0:T(8,128)}, u32[]{:S(2)}, u32[]{:S(2)}) %collective-permute-start.2) | collective-permute-done | bytes 8388640 | tf_op jit(solution)/shard_map/ppermute | solution.py:16
  381.1 0.0 copy-start
  381.1 16.7 %fusion.26 = bf16[1,2,64,1024]{3,2,1,0:T(8,128)(2,1)S(1)} fusion(f32[2,64,2048]{2,1,0:T(8,128)S(1)} %bitcast.68, f32[1,1024,2048]{2,1,0:T(8,128)} %collective-permute-done.2, f32[1,1024,2048]{2,1,0:T(8,128)} %collective-permute-done.1, f32[1,1024,2048]{2,1,0:T(8,128)S(1)} %collective-permute-done, bf16[1024,2048]{1,0:T(8,128)(2,1)} %param.5, ...), kind=kOutput, calls=%fused_computation.32 | convolution fusion | flops 3231842304 | bytes 30679040 | tf_op jit(solution)/shard_map/fin,nc->fci/dot_general | solution.py:29
  397.7 1.0 copy.11
  398.7 363.0 %all-to-all-start = ((bf16[1,2,64,1024]{3,1,0,2:T(2,128)(2,1)}), bf16[1,2,64,1024]{3,1,0,2:T(2,128)(2,1)S(1)}, u32[]{:S(2)}, u32[]{:S(2)}) async-start(bf16[1,2,64,1024]{3,1,0,2:T(2,128)(2,1)} %copy.11), calls=%async_computation | async-start | bytes 524288 | tf_op jit(solution)/shard_map/all_to_all | solution.py:60
  761.7 0.0 copy-done
  761.7 8.2 %all-to-all-done = bf16[1,2,64,1024]{3,1,0,2:T(2,128)(2,1)S(1)} async-done(((bf16[1,2,64,1024]{3,1,0,2:T(2,128)(2,1)}), bf16[1,2,64,1024]{3,1,0,2:T(2,128)(2,1)S(1)}, u32[]{:S(2)}, u32[]{:S(2)}) %all-to-all-start) | async-done | bytes 262176 | tf_op jit(solution)/shard_map/all_to_all | solution.py:60
  769.9 0.1 copy.24
  770.0 2.4 all-gather
  772.4 0.7 gather_fusion.1
  773.1 0.7 gather_fusion
  773.8 1.5 fusion.24
  775.4 0.1 slice_bitcast_fusion.3
  775.5 0.1 slice_bitcast_fusion.1
  775.5 15.9 %multiply_convert_fusion = bf16[8,18,512,256]{3,2,1,0:T(8,128)(2,1)} fusion(bf16[8,8,18,256]{3,0,2,1:T(8,128)(2,1)S(1)} %fusion.37, bf16[8,8,18,256]{3,0,2,1:T(8,128)(2,1)S(1)} %get-tuple-element.16, bf16[8,8,18,256]{3,0,2,1:T(8,128)(2,1)S(1)} %get-tuple-element.15, bf16[8,8,18,256]{3,0,2,1:T(8,128)(2,1)S(1)} %get-tuple-element.14, ...), kind=kOutput, calls=%fused_computation.2 | convolution fusion | flops 653524992 | bytes 40697856 | tf_op jit(solution)/shard_map/sctu,sctv->ctuv/dot_general | solution.py:87
  (5 shorter events, 0.1 us)
Async XLA Ops:
  13.3 184.8 %collective-permute-start = (f32[1,1024,2048]{2,1,0:T(8,128)}, f32[1,1024,2048]{2,1,0:T(8,128)S(1)}, u32[]{:S(2)}, u32[]{:S(2)}) collective-permute-start(f32[1,1024,2048]{2,1,0:T(8,128)} %get-tuple-element.10), channel_id=1, source_target_pairs={{0,2},{2,4},{4,6},{6,8},{8,10},{10,12},{12,14},{1,3},{3,5},{5,7},{... | collective-permute-start | bytes 25165832 | tf_op jit(solution)/shard_map/ppermute | solution.py:16
  18.6 184.2 %collective-permute-start.1 = (f32[1,1024,2048]{2,1,0:T(8,128)}, f32[1,1024,2048]{2,1,0:T(8,128)}, u32[]{:S(2)}, u32[]{:S(2)}) collective-permute-start(f32[1,1024,2048]{2,1,0:T(8,128)} %get-tuple-element.11), channel_id=1, source_target_pairs={{0,4},{2,6},{4,8},{6,10},{8,12},{10,14},{1,5},{3,7},{5,9},{7,11},{... | collective-permute-start | bytes 25165832 | tf_op jit(solution)/shard_map/ppermute | solution.py:16
  24.8 356.3 %collective-permute-start.2 = (f32[1,1024,2048]{2,1,0:T(8,128)}, f32[1,1024,2048]{2,1,0:T(8,128)}, u32[]{:S(2)}, u32[]{:S(2)}) collective-permute-start(f32[1,1024,2048]{2,1,0:T(8,128)} %get-tuple-element.12), channel_id=1, source_target_pairs={{0,6},{2,8},{4,10},{6,12},{8,14},{1,7},{3,9},{5,11},{7,13},{9,15},... | collective-permute-start | bytes 25165832 | tf_op jit(solution)/shard_map/ppermute | solution.py:16
  381.1 380.6 %copy-start = (s32[18,2]{0,1:T(2,128)S(1)}, s32[18,2]{0,1:T(2,128)}, u32[]{:S(2)}) copy-start(s32[18,2]{0,1:T(2,128)} %param.7) | copy-start | bytes 436
  398.7 371.2 %all-to-all-start = ((bf16[1,2,64,1024]{3,1,0,2:T(2,128)(2,1)}), bf16[1,2,64,1024]{3,1,0,2:T(2,128)(2,1)S(1)}, u32[]{:S(2)}, u32[]{:S(2)}) async-start(bf16[1,2,64,1024]{3,1,0,2:T(2,128)(2,1)} %copy.11), calls=%async_computation | async-start | bytes 524288 | tf_op jit(solution)/shard_map/all_to_all | solution.py:60
where the time goes:
time: 792 us; the launch traced here: 791 us
  starting transfers between devices  379 us (48%)
  waiting for transfers between devices  358 us (45%)
  matrix products  32.6 us (4%)
  other arithmetic  16.1 us (2%)
    all_to_all x1, starting transfers between devices, corner_turn(): lax.all_to_all(spectra.astype(jnp.bfloat16), 'tm', split_axis=2, concat_a...  363 us
    ppermute x3, waiting for transfers between devices, shifted(): return lax.ppermute(array, axis, pairs)  350 us
    dot_general x1, matrix products, transform(): jnp.einsum('fin,nc->fci', frame_block, cosine_table, precision=lax.Precis...  16.7 us
    ppermute x3, starting transfers between devices, shifted(): return lax.ppermute(array, axis, pairs)  16 us
    dot_general x1, matrix products, local(): jnp.einsum('sctu,sctv->ctuv', combined, stacked_right, preferred_element_...  15.9 us
  transfers between devices with their start and end apart: 4, of which 4 were waited for; matrix products, arithmetic and copies ran while one was open for 0% of the time, Pallas kernels for 0%

commit v1 on v0

v1 whole, which is shorter than its diff:
```python
import functools

import jax
import jax.numpy as jnp
import numpy as np
from jax import lax
from jax.experimental import pallas as pl
from jax.experimental.pallas import tpu as pltpu
from jax.sharding import PartitionSpec as P

INPUTS = 2048
NFFT = 2048
TAPS = 4
CHAN = 64
TILE = 256
NB = INPUTS // TILE

CHUNKS = 1


def basis_rows(owners, first, count):
    per_owner = CHAN // owners
    chan = np.arange(owners)[:, None] * per_owner + first + np.arange(count)[None, :]
    wrapped = (np.arange(NFFT, dtype=np.int64)[None, :] * (CHAN + chan.reshape(-1, 1))) % NFFT
    angle = wrapped.astype(np.float64) * (2.0 * np.pi / NFFT)
    both = np.stack([np.cos(angle), -np.sin(angle)], axis=1) / np.sqrt(NFFT)
    return both.reshape(-1, NFFT).astype(np.float32)


def tap_sum(owners, count):
    matrix = np.zeros((count, 2, owners, owners, TAPS, count, 2), np.float32)
    for frame in range(owners):
        for tap in range(min(TAPS, frame + 1)):
            for chan in range(count):
                for part in range(2):
                    matrix[chan, part, frame, frame - tap, tap, chan, part] = 1.0
    return matrix.reshape(count * 2 * owners, -1)


def left_factors(owners, count):
    depth = count * 2 * owners
    real = np.zeros((count, 2, owners, count, 2, owners), np.float32)
    imag = np.zeros((count, 2, owners, count, 2, owners), np.float32)
    for chan in range(count):
        for frame in range(owners):
            real[chan, 0, frame, chan, 0, frame] = 1.0 / owners
            real[chan, 1, frame, chan, 1, frame] = 1.0 / owners
            imag[chan, 1, frame, chan, 0, frame] = 1.0 / owners
            imag[chan, 0, frame, chan, 1, frame] = -1.0 / owners
    return np.stack([real.reshape(depth, depth), imag.reshape(depth, depth)])


def transform_kernel(group, basis_ref, window_ref, samples_ref, out_ref, high, low):
    @pl.when(pl.program_id(0) == 0)
    def _():
        for first in range(0, basis_ref.shape[0], group):
            basis = basis_ref[first : first + group, :]
            weights = jnp.concatenate([basis * window_ref[k : k + 1, :] for k in range(TAPS)], axis=0)
            rounded = weights.astype(jnp.bfloat16)
            rows = pl.ds(first * TAPS, group * TAPS)
            high[rows, :] = rounded
            low[rows, :] = (weights - rounded.astype(jnp.float32)).astype(jnp.bfloat16)

    contract = (((1,), (1,)), ((), ()))
    samples = samples_ref[...]
    total = lax.dot_general(high[...], samples, contract, preferred_element_type=jnp.float32)
    total += lax.dot_general(low[...], samples, contract, preferred_element_type=jnp.float32)
    out_ref[...] = total.astype(out_ref.dtype)


def transform(samples, window, owners, first, count):
    inputs = samples.shape[0]
    basis = basis_rows(owners, first, count)
    rows = basis.shape[0]
    cols = 2 * count
    together = 1 if cols % 8 == 0 else 8 // cols
    group = cols * together
    block = 256
    out = pl.pallas_call(
        functools.partial(transform_kernel, group),
        grid=(inputs // block,),
        in_specs=[
            pl.BlockSpec((rows, NFFT), lambda i: (0, 0)),
            pl.BlockSpec((TAPS, NFFT), lambda i: (0, 0)),
            pl.BlockSpec((block, NFFT), lambda i: (i, 0)),
        ],
        out_specs=pl.BlockSpec((rows * TAPS, block), lambda i: (0, i)),
        out_shape=jax.ShapeDtypeStruct((rows * TAPS, inputs), jnp.bfloat16),
        scratch_shapes=[pltpu.VMEM((rows * TAPS, NFFT), jnp.bfloat16)] * 2,
        compiler_params=pltpu.CompilerParams(vmem_limit_bytes=48 << 20),
    )(jnp.asarray(basis), window, samples)
    if together > 1:
        out = out.reshape(owners // together, TAPS, together, cols, inputs)
        out = jnp.transpose(out, (0, 2, 1, 3, 4))
    return out.reshape(owners, TAPS * cols, inputs)


def power_kernel(count, table_ref, where_ref, own_ref, other_ref, left_ref, out_ref, left, right):
    depth = own_ref.shape[0]
    half = NB // 2

    @pl.when(pl.program_id(0) == 0)
    def _():
        chan = lax.broadcasted_iota(jnp.int32, (depth, TILE), 0) // (depth // count)
        for index in range(NB):
            ref = own_ref if index < half else other_ref
            base = where_ref[0] if index < half else half - where_ref[0]
            place = base + index % half
            piece = ref[:, (index % half) * TILE : (index % half + 1) * TILE]
            for part in range(2):
                turned = lax.dot_general(
                    piece, left_ref[part], (((0,), (0,)), ((), ())), preferred_element_type=jnp.float32
                )
                left[place, part * TILE : (part + 1) * TILE, :] = turned.astype(jnp.bfloat16)
            for c in range(count):
                right[place, c] = jnp.where(chan == c, piece, jnp.zeros_like(piece))

    j = pl.program_id(0)
    first = left[table_ref[j, 0]]
    q = table_ref[j, 1]
    for c in range(count):
        power = jnp.dot(first, right[q, c], preferred_element_type=jnp.float32)
        out_ref[c, 0] = power.astype(jnp.bfloat16).reshape(2, TILE, TILE)


def cross_power(table, where, own, other, count, total, chunk, previous):
    depth, width = own.shape
    tiles = table.shape[0]
    owners = depth // (2 * count)
    whole = lambda j, *_: (0, 0)
    in_specs = [
        pl.BlockSpec((depth, width), whole),
        pl.BlockSpec((depth, width), whole),
        pl.BlockSpec((2, depth, depth), lambda j, *_: (0, 0, 0)),
    ]
    args = [table, where, own, other, jnp.asarray(left_factors(owners, count), jnp.bfloat16)]
    kernel = functools.partial(power_kernel, count)
    aliases = {}
    if previous is not None:
        in_specs.append(pl.BlockSpec(memory_space=pl.ANY))
        args.append(previous)
        aliases = {5: 0}
        inner = kernel
        kernel = lambda t, w, a, b, l, _, o, left, right: inner(t, w, a, b, l, o, left, right)
    return pl.pallas_call(
        kernel,
        grid_spec=pltpu.PrefetchScalarGridSpec(
            num_scalar_prefetch=2,
            grid=(tiles,),
            in_specs=in_specs,
            out_specs=pl.BlockSpec((count, 1, 2, TILE, TILE), lambda j, *_: (chunk, j, 0, 0, 0)),
            scratch_shapes=[
                pltpu.VMEM((NB, 2 * TILE, depth), jnp.bfloat16),
                pltpu.VMEM((NB, count, depth, TILE), jnp.bfloat16),
            ],
        ),
        out_shape=jax.ShapeDtypeStruct((total, tiles, 2, TILE, TILE), jnp.bfloat16),
        input_output_aliases=aliases,
        compiler_params=pltpu.CompilerParams(vmem_limit_bytes=48 << 20),
    )(*args)


def local(raw_samples, pfb_window, tile_table):
    owners = lax.axis_size("tm")
    inputs = raw_samples.shape[0]
    total = CHAN // owners
    chunks = CHUNKS if total % CHUNKS == 0 else 1
    count = total // chunks
    where = (lax.axis_index("inp") * (NB // 2)).astype(jnp.int32).reshape(1)
    turned = []
    for chunk in range(chunks):
        partial = transform(raw_samples, pfb_window, owners, chunk * count, count)
        turned.append(lax.all_to_all(partial, "tm", split_axis=0, concat_axis=0, tiled=True))
    out = None
    for chunk in range(chunks):
        add = jnp.asarray(tap_sum(owners, count), jnp.bfloat16)
        own = jnp.dot(add, turned[chunk].reshape(-1, inputs), preferred_element_type=jnp.float32)
        own = own.astype(jnp.bfloat16)
        other = lax.ppermute(own, "inp", [(0, 1), (1, 0)])
        out = cross_power(tile_table, where, own, other, count, total, chunk, out)
    return out


def solution(mesh):
    return jax.shard_map(
        local,
        mesh=mesh,
        in_specs=(P(("grp", "inp"), "tm"), P(), P("inp", None)),
        out_specs=P(("grp", "tm"), "inp", None, None, None),
        check_vma=False,
    )
```

time: 792 us -> 66.3 us (0.08)
  starting transfers between devices: 379 us -> 0.07 us
  waiting for transfers between devices: 358 us -> 0.75 us
  matrix products: 32.6 us -> 1.21 us
  blocking collectives: 2.4 us -> 32.8 us
  Pallas kernels: 0 us -> 27.4 us
  other arithmetic: 16.1 us -> 0 us
    all_to_all x1 -> x0, starting transfers between devices: 363 us -> none  [corner_turn(): lax.all_to_all(spectra.astype(jnp.bfloat16), 'tm', split_axis=2, concat_a...]
    ppermute x3 -> x1, waiting for transfers between devices: 350 us -> 0.75 us  [local(): other = lax.ppermute(own, 'inp', [(0, 1), (1, 0)])]
    all_to_all x0 -> x1, blocking collectives: none -> 32.8 us  [local(): lax.all_to_all(partial, 'tm', split_axis=0, concat_axis=0, tiled=True)]
    dot_general x2 -> x1, matrix products: 32.6 us -> 1.21 us  [local(): jnp.dot(add, turned[chunk].reshape(-1, inputs), preferred_element_type=jn...]
    pallas_call x0 -> x2, Pallas kernels: none -> 27.4 us  [the longest x1 20.1 us: cross_power(): pl.pallas_call(kernel, grid_spec=pltpu.PrefetchScalarGridSpec(num_scalar_...]
    ppermute x3 -> x1, starting transfers between devices: 16 us -> 0.07 us  [local(): other = lax.ppermute(own, 'inp', [(0, 1), (1, 0)])]
    another operation x1 -> x0, other arithmetic: 12.3 us -> none  [filter_pieces(): outgoing.append(jnp.stack(partial_list))]
    all_to_all x1 -> x0, waiting for transfers between devices: 8.18 us -> none  [corner_turn(): lax.all_to_all(spectra.astype(jnp.bfloat16), 'tm', split_axis=2, concat_a...]
  transfers between devices with their start and end apart: 4 -> 1, of which waited for: 4 -> 1; matrix products, arithmetic and copies ran while one was open for 0% -> 1% of each run, Pallas kernels for 0% -> 0%
where the time goes in v1:
time: 66.3 us; the launch traced here: 65.9 us
  blocking collectives  32.8 us (49%)
  Pallas kernels  27.4 us (41%)
  local copies, waits for them, and re-layouts  3.59 us (5%)
  matrix products  1.21 us (2%)
  waiting for transfers between devices  0.75 us (1%)
    all_to_all x1, blocking collectives, local(): lax.all_to_all(partial, 'tm', split_axis=0, concat_axis=0, tiled=True)  32.8 us
    pallas_call x1, Pallas kernels, cross_power(): pl.pallas_call(kernel, grid_spec=pltpu.PrefetchScalarGridSpec(num_scalar_...  20.1 us
    pallas_call x1, Pallas kernels, transform(): pl.pallas_call(functools.partial(transform_kernel, group), grid=(inputs /...  7.28 us
    unnamed x7, local copies, waits for them, and re-layouts  3.59 us
  transfers between devices with their start and end apart: 1, of which 1 were waited for; matrix products, arithmetic and copies ran while one was open for 1% of the time, Pallas kernels for 0%

profile of v1, /device:TPU:0, one launch (start us, length us, event | category | flops | bytes accessed | tf_op | source)
XLA Modules:
  0.0 65.9 jit_solution(4126673141413914621)
XLA Ops:
  0.0 0.0 copy-start
  0.0 1.2 %copy-done = f32[128,2048]{1,0:T(8,128)S(1)} copy-done((f32[128,2048]{1,0:T(8,128)S(1)}, f32[128,2048]{1,0:T(8,128)}, u32[]{:S(2)}) %copy-start) | copy-done | bytes 1048600
  1.2 0.0 copy-start.2
  1.2 0.8 %copy-done.2 = f32[4,2048]{1,0:T(4,128)S(1)} copy-done((f32[4,2048]{1,0:T(4,128)S(1)}, f32[4,2048]{1,0:T(4,128)}, u32[]{:S(2)}) %copy-start.2) | copy-done | bytes 32792
  2.0 7.3 %shard_map.64 = bf16[512,1024]{1,0:T(8,128)(2,1)S(1)} custom-call(f32[128,2048]{1,0:T(8,128)S(1)} %copy-done, f32[4,2048]{1,0:T(4,128)S(1)} %copy-done.2, bf16[1024,2048]{1,0:T(8,128)(2,1)} %samples_ref.1), custom_call_target="tpu_custom_call" | custom-call | tf_op jit(solution)/shard_map/pallas_call | solution.py:79
  9.3 32.8 %all_to_all.5 = bf16[8,64,1024]{2,1,0:T(8,128)(2,1)S(1)} all-to-all(bf16[8,64,1024]{2,1,0:T(8,128)(2,1)S(1)} %bitcast.7), channel_id=1, replica_groups=mesh['grp'=2,'tm'=8,'inp'=2] {'tm'}, dimensions={0} | all-to-all | bytes 2097152 | tf_op jit(solution)/shard_map/all_to_all | solution.py:173
  42.1 1.2 %fusion.own_ref = bf16[128,1024]{1,0:T(8,128)(2,1)S(1)} fusion(bf16[128,512]{1,0:T(8,128)(2,1)} %constant.13.clone, bf16[512,1024]{1,0:T(8,128)(2,1)S(1)} %bitcast.8), kind=kOutput, calls=%fused_computation.1 | convolution fusion | flops 134348800 | bytes 1441792 | tf_op jit(solution)/shard_map/dot_general | solution.py:177
  43.3 0.1 collective-permute-start
  43.4 0.8 %copy.8.table_ref = s32[18,2]{1,0:T(8,128)S(1)} copy(s32[18,2]{0,1:T(2,128)} %param.8) | data formatting | bytes 288 | tf_op args[2]
  44.2 0.7 %collective-permute-done.other_ref = bf16[128,1024]{1,0:T(8,128)(2,1)S(1)} collective-permute-done((bf16[128,1024]{1,0:T(8,128)(2,1)S(1)}, bf16[128,1024]{1,0:T(8,128)(2,1)S(1)}, u32[]{:S(2)}, u32[]{:S(2)}) %collective-permute-start) | collective-permute-done | bytes 262176 | tf_op jit(solution)/shard_map/ppermute | solution.py:179
  44.9 0.0 copy-start.1
  44.9 0.8 %copy-done.1 = bf16[2,128,128]{2,1,0:T(8,128)(2,1)S(1)} copy-done((bf16[2,128,128]{2,1,0:T(8,128)(2,1)S(1)}, bf16[2,128,128]{2,1,0:T(8,128)(2,1)}, u32[]{:S(2)}) %copy-start.1) | copy-done | bytes 65560
  45.8 20.1 %shard_map.65 = bf16[8,18,2,256,256]{4,3,2,1,0:T(8,128)(2,1)} custom-call(s32[18,2]{1,0:T(8,128)S(1)} %copy.8.table_ref, s32[1]{0:T(128)} %bitcast.where_ref, bf16[128,1024]{1,0:T(8,128)(2,1)S(1)} %fusion.own_ref, bf16[128,1024]{1,0:T(8,128)(2,1)S(1)} %collective-permute-done.other_ref, bf16[2,128,128]{2,1,0:T(8,128)(2,1)S(1)} %copy-done.1), custom_call_target="tpu_custom_call" | custom-call | tf_op jit(solution)/shard_map/pallas_call | solution.py:145
Async XLA Ops:
  0.0 1.2 %copy-start = (f32[128,2048]{1,0:T(8,128)S(1)}, f32[128,2048]{1,0:T(8,128)}, u32[]{:S(2)}) copy-start(f32[128,2048]{1,0:T(8,128)} %constant.12.clone.basis_ref) | copy-start | bytes 3145732
  1.2 0.8 %copy-start.2 = (f32[4,2048]{1,0:T(4,128)S(1)}, f32[4,2048]{1,0:T(4,128)}, u32[]{:S(2)}) copy-start(f32[4,2048]{1,0:T(4,128)} %window_ref.1) | copy-start | bytes 98308
  43.3 1.6 %collective-permute-start = (bf16[128,1024]{1,0:T(8,128)(2,1)S(1)}, bf16[128,1024]{1,0:T(8,128)(2,1)S(1)}, u32[]{:S(2)}, u32[]{:S(2)}) collective-permute-start(bf16[128,1024]{1,0:T(8,128)(2,1)S(1)} %fusion.own_ref), channel_id=1, source_target_pairs={{0,1},{1,0},{2,3},{3,2},{4,5},{5,4},{6,7},{7,6},{8,9},{9,8},{10,11... | collective-permute-start | bytes 786440 | tf_op jit(solution)/shard_map/ppermute | solution.py:179
  44.9 0.8 %copy-start.1 = (bf16[2,128,128]{2,1,0:T(8,128)(2,1)S(1)}, bf16[2,128,128]{2,1,0:T(8,128)(2,1)}, u32[]{:S(2)}) copy-start(bf16[2,128,128]{2,1,0:T(8,128)(2,1)} %constant.14.clone.left_ref) | copy-start | bytes 196612

commit v2 on v0

v2 whole, which is shorter than its diff:
```python
import functools

import jax
import jax.numpy as jnp
import numpy as np
from jax import lax
from jax.experimental import pallas as pl
from jax.experimental.pallas import tpu as pltpu
from jax.sharding import PartitionSpec as P

INPUTS = 2048
NFFT = 2048
TAPS = 4
CHAN = 64
TILE = 256
NB = INPUTS // TILE
HALF = NB // 2


def params(mib):
    return pltpu.CompilerParams(vmem_limit_bytes=mib << 20)


def cost(flops, moved):
    return pl.CostEstimate(flops=flops, transcendentals=0, bytes_accessed=moved)


def basis_rows(owners, first, count):
    per_owner = CHAN // owners
    chan = np.arange(owners)[:, None] * per_owner + first + np.arange(count)[None, :]
    wrapped = (np.arange(NFFT, dtype=np.int64)[None, :] * (CHAN + chan.reshape(-1, 1))) % NFFT
    angle = wrapped.astype(np.float64) * (2.0 * np.pi / NFFT)
    both = np.stack([np.cos(angle), -np.sin(angle)], axis=1) / np.sqrt(NFFT)
    return both.reshape(-1, NFFT).astype(np.float32)


def transform_kernel(group, segments, basis_hbm, window_hbm, samples_hbm, *refs):
    *out_refs, basis, window, samples, high, low, sems = refs
    blocks = 2
    size = samples.shape[0] // blocks
    copies = [
        pltpu.make_async_copy(basis_hbm, basis, sems.at[0]),
        pltpu.make_async_copy(window_hbm, window, sems.at[1]),
    ]
    for b in range(blocks):
        rows = pl.ds(b * size, size)
        copies.append(pltpu.make_async_copy(samples_hbm.at[rows], samples.at[rows], sems.at[2 + b]))
    for copy in copies:
        copy.start()
    copies[0].wait()
    copies[1].wait()
    for index, (chunk, distance) in enumerate(segments):
        place = distance
        if len(out_refs) > 1:
            place = lax.bitwise_xor(lax.axis_index("tm"), distance)
        rows = basis[chunk, pl.ds(pl.multiple_of(place * group, group), group), :]
        weights = jnp.concatenate([rows * window[k : k + 1, :] for k in range(TAPS)], axis=0)
        rounded = weights.astype(jnp.bfloat16)
        where = pl.ds(index * group * TAPS, group * TAPS)
        high[where, :] = rounded
        low[where, :] = (weights - rounded.astype(jnp.float32)).astype(jnp.bfloat16)

    contract = (((1,), (1,)), ((), ()))
    for b in range(blocks):
        copies[2 + b].wait()
        piece = samples[b * size : (b + 1) * size, :]
        total = lax.dot_general(high[...], piece, contract, preferred_element_type=jnp.float32)
        total += lax.dot_general(low[...], piece, contract, preferred_element_type=jnp.float32)
        total = total.astype(jnp.bfloat16)
        first = 0
        for out_ref in out_refs:
            out_ref[:, b * size : (b + 1) * size] = total[first : first + out_ref.shape[0]]
            first += out_ref.shape[0]


def transform(samples, window, owners, chunks, count, group, segments, outs):
    inputs = samples.shape[0]
    basis = np.stack([basis_rows(owners, chunk * count, count) for chunk in range(chunks)])
    rows = len(segments) * group * TAPS
    hbm = pl.BlockSpec(memory_space=pl.ANY)
    return pl.pallas_call(
        functools.partial(transform_kernel, group, segments),
        in_specs=[hbm] * 3,
        out_specs=[pl.BlockSpec(memory_space=pltpu.VMEM)] * len(outs),
        out_shape=[jax.ShapeDtypeStruct((n * group * TAPS, inputs), jnp.bfloat16) for n in outs],
        scratch_shapes=[
            pltpu.VMEM(basis.shape, jnp.float32),
            pltpu.VMEM((TAPS, NFFT), jnp.float32),
            pltpu.VMEM((inputs, NFFT), jnp.bfloat16),
            pltpu.VMEM((rows, NFFT), jnp.bfloat16),
            pltpu.VMEM((rows, NFFT), jnp.bfloat16),
            pltpu.SemaphoreType.DMA((4,)),
        ],
        compiler_params=params(60),
        cost_estimate=cost(4 * rows * inputs * NFFT, 8 << 20),
    )(jnp.asarray(basis), window, samples)


def tap_matrix(frames, pieces, count, first):
    cols = 2 * count
    shape = (cols * frames, pieces * TAPS * cols)
    row = lax.broadcasted_iota(jnp.int32, shape, 0)
    col = lax.broadcasted_iota(jnp.int32, shape, 1)
    source = lax.bitwise_xor(col // (TAPS * cols), first)
    hit = (col % cols == row // frames) & (row % frames - (col // cols) % TAPS == source)
    return jnp.where(hit, 1.0, 0.0).astype(jnp.bfloat16)


def tap_sum_kernel(owners, count, spectra_ref, out_ref):
    add = tap_matrix(owners, owners, count, 0)
    out_ref[...] = jnp.dot(add, spectra_ref[...], preferred_element_type=jnp.float32).astype(jnp.bfloat16)


def near_sum_kernel(owners, count, *refs):
    *parts, near_first, near_second, facing = refs
    depth = TAPS * 2 * count
    add = tap_matrix(owners, owners // 2, count, lax.axis_index("tm"))
    for index, out_ref in enumerate((near_first, near_second, facing)):
        spectra = jnp.concatenate([ref[index * depth : (index + 1) * depth, :] for ref in parts], axis=0)
        total = jnp.dot(add, spectra, preferred_element_type=jnp.float32)
        out_ref[...] = total.astype(out_ref.dtype)


def far_sum_kernel(owners, count, near_ref, *refs):
    *parts, out_ref = refs
    half = owners // 2
    add = tap_matrix(owners, half, count, lax.bitwise_xor(lax.axis_index("tm"), half))
    spectra = jnp.concatenate([ref[...] for ref in parts], axis=0)
    total = near_ref[...] + jnp.dot(add, spectra, preferred_element_type=jnp.float32)
    out_ref[...] = total.astype(jnp.bfloat16)


def join_kernel(near_ref, far_ref, out_ref):
    out_ref[...] = (near_ref[...] + far_ref[...].astype(jnp.float32)).astype(jnp.bfloat16)


def small(kernel, outs, inputs):
    vmem = pl.BlockSpec(memory_space=pltpu.VMEM)
    return pl.pallas_call(
        kernel,
        in_specs=[vmem] * len(inputs),
        out_specs=[vmem] * len(outs),
        out_shape=outs,
        compiler_params=params(16),
        cost_estimate=cost(1 << 28, 1 << 20),
    )(*inputs)


def power_kernel(count, chunk, together, table_ref, own_ref, other_ref, *refs):
    out_ref, left, right, buf, sem = refs[-5:]
    depth = own_ref.shape[0]
    frames = depth // (2 * count)
    slots = buf.shape[0]
    steps = out_ref.shape[1] // together
    mine = lax.axis_index("inp") * HALF

    row = lax.broadcasted_iota(jnp.int32, (depth, depth), 0)
    col = lax.broadcasted_iota(jnp.int32, (depth, depth), 1)
    scale = 1.0 / frames
    real = jnp.where(row == col, scale, 0.0).astype(jnp.bfloat16)
    sign = jnp.where((col // frames) % 2 == 0, scale, -scale)
    partner = (row // (2 * frames) == col // (2 * frames)) & (row % frames == col % frames)
    imag = jnp.where(partner & (row != col), sign, 0.0).astype(jnp.bfloat16)
    chan = lax.broadcasted_iota(jnp.int32, (depth, TILE), 0) // (2 * frames)
    for index in range(NB):
        ref = own_ref if index < HALF else other_ref
        place = (mine if index < HALF else HALF - mine) + index % HALF
        piece = ref[:, (index % HALF) * TILE : (index % HALF + 1) * TILE]
        for part, turn in enumerate((real, imag)):
            turned = lax.dot_general(piece, turn, (((0,), (0,)), ((), ())), preferred_element_type=jnp.float32)
            left[place, part * TILE : (part + 1) * TILE, :] = turned.astype(jnp.bfloat16)
        for c in range(count):
            right[place, c] = jnp.where(chan == c, piece, jnp.zeros_like(piece))

    def copy(step):
        slot = lax.rem(step, slots)
        where = out_ref.at[pl.ds(chunk * count, count), pl.ds(step * together, together)]
        return pltpu.make_async_copy(buf.at[slot], where, sem.at[slot])

    def body(step, carry):
        slot = lax.rem(step, slots)

        @pl.when(step >= slots)
        def _():
            copy(step - slots).wait()

        for u in range(together):
            p = table_ref[step * together + u, 0]
            q = table_ref[step * together + u, 1]
            for c in range(count):
                for part in range(2):
                    first = left[p, part * TILE : (part + 1) * TILE, :]
                    power = jnp.dot(first, right[q, c], preferred_element_type=jnp.float32)
                    buf[slot, c, u, part] = power.astype(jnp.bfloat16)
        copy(step).start()
        return carry

    lax.fori_loop(0, steps, body, 0)

    def drain(step, carry):
        copy(step).wait()
        return carry

    lax.fori_loop(steps - slots, steps, drain, 0)


def cross_power(table, own, other, count, total, chunk, previous):
    depth, width = own.shape
    tiles = table.shape[0]
    together = 2 if tiles % 2 == 0 else 1
    vmem = pl.BlockSpec(memory_space=pltpu.VMEM)
    hbm = pl.BlockSpec(memory_space=pl.ANY)
    in_specs = [pl.BlockSpec(memory_space=pltpu.SMEM), vmem, vmem]
    args = [table, own, other]
    aliases = {}
    if previous is not None:
        in_specs.append(hbm)
        args.append(previous)
        aliases = {3: 0}
    return pl.pallas_call(
        functools.partial(power_kernel, count, chunk, together),
        in_specs=in_specs,
        out_specs=hbm,
        out_shape=jax.ShapeDtypeStruct((total, tiles, 2, TILE, TILE), jnp.bfloat16),
        scratch_shapes=[
            pltpu.VMEM((NB, 2 * TILE, depth), jnp.bfloat16),
            pltpu.VMEM((NB, count, depth, TILE), jnp.bfloat16),
            pltpu.VMEM((3, count, together, 2, TILE, TILE), jnp.bfloat16),
            pltpu.SemaphoreType.DMA((3,)),
        ],
        input_output_aliases=aliases,
        compiler_params=params(24),
        cost_estimate=cost(2 * tiles * count * 2 * TILE * TILE * 256, tiles * count * 4 * TILE * TILE),
    )(*args)


def finish(table, own, count, total, chunk, out):
    other = lax.ppermute(own, "inp", [(0, 1), (1, 0)])
    return cross_power(table, own, other, count, total, chunk, out)


def turn_whole(samples, window, table, owners, total):
    inputs = samples.shape[0]
    cols = 2 * total
    together = 1 if cols % 8 == 0 else 8 // cols
    group = cols * together
    segments = [(0, d) for d in range(owners // together)]
    (partial,) = transform(samples, window, owners, 1, total, group, segments, [len(segments)])
    partial = partial.reshape(owners // together, TAPS, together, cols, inputs)
    partial = jnp.transpose(partial, (0, 2, 1, 3, 4)).reshape(owners, TAPS * cols, inputs)
    turned = lax.all_to_all(partial, "tm", split_axis=0, concat_axis=0, tiled=True)
    kernel = functools.partial(tap_sum_kernel, owners, total)
    sums = jax.ShapeDtypeStruct((cols * owners, inputs), jnp.bfloat16)
    (own,) = small(kernel, [sums], [turned.reshape(-1, inputs)])
    return finish(table, own, total, total, 0, None)


def local(raw_samples, pfb_window, tile_table):
    owners = lax.axis_size("tm")
    total = CHAN // owners
    if owners != 8:
        return turn_whole(raw_samples, pfb_window, tile_table, owners, total)

    inputs = raw_samples.shape[0]
    count = total // 2
    half = owners // 2
    segments = [(0, half + d) for d in range(half)]
    for d in range(half):
        segments += [(0, d), (1, d), (1, half + d)]
    outs = [1] * half + [3] * half
    sent = transform(raw_samples, pfb_window, owners, 2, count, 2 * count, segments, outs)

    def swap(block, d):
        return block if d == 0 else lax.ppermute(block, "tm", [(i, i ^ d) for i in range(owners)])

    far = [swap(sent[d], half + d) for d in range(half)]
    near = [swap(sent[half + d], d) for d in range(half)]
    exact = jax.ShapeDtypeStruct((2 * count * owners, inputs), jnp.float32)
    rounded = jax.ShapeDtypeStruct((2 * count * owners, inputs), jnp.bfloat16)
    kernel = functools.partial(near_sum_kernel, owners, count)
    near_first, near_second, facing = small(kernel, [exact, exact, rounded], near)
    faced = swap(facing, half)
    kernel = functools.partial(far_sum_kernel, owners, count)
    (own,) = small(kernel, [rounded], [near_first] + far)
    out = finish(tile_table, own, count, total, 0, None)
    faced, out = lax.optimization_barrier((faced, out))
    (own,) = small(join_kernel, [rounded], [near_second, faced])
    return finish(tile_table, own, count, total, 1, out)


def solution(mesh):
    return jax.shard_map(
        local,
        mesh=mesh,
        in_specs=(P(("grp", "inp"), "tm"), P(), P("inp", None)),
        out_specs=P(("grp", "tm"), "inp", None, None, None),
        check_vma=False,
    )
```

time: 792 us -> 50.3 us (0.06)
  starting transfers between devices: 379 us -> 17.9 us
  waiting for transfers between devices: 358 us -> 4.84 us
  matrix products: 32.6 us -> 0 us
  Pallas kernels: 0 us -> 25.5 us
  other arithmetic: 16.1 us -> 0 us
    all_to_all x1 -> x0, starting transfers between devices: 363 us -> none  [corner_turn(): lax.all_to_all(spectra.astype(jnp.bfloat16), 'tm', split_axis=2, concat_a...]
    ppermute x3 -> x10, waiting for transfers between devices: 350 us -> 4.84 us  [the longest x8 3.71 us: swap(): lax.ppermute(block, 'tm', [(i, i ^ d) for i in range(owners)])]
    dot_general x2 -> x0, matrix products: 32.6 us -> none  [the longest x1 16.7 us: transform(): jnp.einsum('fin,nc->fci', frame_block, cosine_table, precision=lax.Precis...]
    pallas_call x0 -> x6, Pallas kernels: none -> 25.5 us  [the longest x2 17.5 us: cross_power(): pl.pallas_call(functools.partial(power_kernel, count, chunk, together), i...]
    another operation x1 -> x0, other arithmetic: 12.3 us -> none  [filter_pieces(): outgoing.append(jnp.stack(partial_list))]
    all_to_all x1 -> x0, waiting for transfers between devices: 8.18 us -> none  [corner_turn(): lax.all_to_all(spectra.astype(jnp.bfloat16), 'tm', split_axis=2, concat_a...]
    ppermute x3 -> x10, starting transfers between devices: 16 us -> 17.9 us  [the longest x8 17.5 us: swap(): lax.ppermute(block, 'tm', [(i, i ^ d) for i in range(owners)])]
  transfers between devices with their start and end apart: 4 -> 10, of which waited for: 4 -> 4; matrix products, arithmetic and copies ran while one was open for 0% -> 2% of each run, Pallas kernels for 0% -> 18%
where the time goes in v2:
time: 50.3 us; the launch traced here: 50 us
  Pallas kernels  25.5 us (51%)
  starting transfers between devices  17.9 us (36%)
  waiting for transfers between devices  4.84 us (10%)
  local copies, waits for them, and re-layouts  1.7 us (3%)
    ppermute x8, starting transfers between devices, swap(): lax.ppermute(block, 'tm', [(i, i ^ d) for i in range(owners)])  17.5 us
    pallas_call x2, Pallas kernels, cross_power(): pl.pallas_call(functools.partial(power_kernel, count, chunk, together), i...  17.5 us
    pallas_call x1, Pallas kernels, transform(): pl.pallas_call(functools.partial(transform_kernel, group, segments), in_s...  7.52 us
    ppermute x8, waiting for transfers between devices, swap(): lax.ppermute(block, 'tm', [(i, i ^ d) for i in range(owners)])  3.71 us
    unnamed x3, local copies, waits for them, and re-layouts  1.7 us
    ppermute x2, waiting for transfers between devices, finish(): other = lax.ppermute(own, 'inp', [(0, 1), (1, 0)])  1.13 us
  transfers between devices with their start and end apart: 10, of which 4 were waited for; matrix products, arithmetic and copies ran while one was open for 2% of the time, Pallas kernels for 18%

profile of v2, /device:TPU:0, one launch (start us, length us, event | category | flops | bytes accessed | tf_op | source)
XLA Modules:
  0.0 50.0 jit_solution(1276597593291521006)
XLA Ops:
  0.0 7.5 %shard_map.46 = (bf16[32,1024]{1,0:T(8,128)(2,1)}, bf16[32,1024]{1,0:T(8,128)(2,1)}, bf16[32,1024]{1,0:T(8,128)(2,1)}, bf16[32,1024]{1,0:T(8,128)(2,1)}, bf16[96...) custom-call(f32[2,64,2048]{2,1,0:T(8,128)} %constant.2.clone.basis_hbm, ...), custom_call_target="tpu_custom_call" | custom-call | flops 4294967296 | bytes 8388608 | tf_op jit(solution)/shard_map/pallas_call | solution.py:81
  7.5 3.0 %collective-permute-start = (bf16[96,1024]{1,0:T(8,128)(2,1)}, bf16[96,1024]{1,0:T(8,128)(2,1)S(1)}, u32[]{:S(2)}, u32[]{:S(2)}) collective-permute-start(bf16[96,1024]{1,0:T(8,128)(2,1)} %get-tuple-element.19), channel_id=1, source_target_pairs={{0,2},{2,0},{4,6},{6,4},{8,10},{10,8},{12,14},{14,12},{1,3},{3,1},... | collective-permute-start | bytes 589832 | tf_op jit(solution)/shard_map/ppermute | solution.py:274
  10.5 1.6 %collective-permute-start.1 = (bf16[96,1024]{1,0:T(8,128)(2,1)}, bf16[96,1024]{1,0:T(8,128)(2,1)S(1)}, u32[]{:S(2)}, u32[]{:S(2)}) collective-permute-start(bf16[96,1024]{1,0:T(8,128)(2,1)} %get-tuple-element.20), channel_id=1, source_target_pairs={{0,4},{2,6},{4,0},{6,2},{8,12},{10,14},{12,8},{14,10},{1,5},{3,7},... | collective-permute-start | bytes 589832 | tf_op jit(solution)/shard_map/ppermute | solution.py:274
  12.1 0.0 collective-permute-start.2
  12.1 3.0 %collective-permute-start.4 = (bf16[32,1024]{1,0:T(8,128)(2,1)}, bf16[32,1024]{1,0:T(8,128)(2,1)S(1)}, u32[]{:S(2)}, u32[]{:S(2)}) collective-permute-start(bf16[32,1024]{1,0:T(8,128)(2,1)} %get-tuple-element.25), channel_id=1, source_target_pairs={{0,8},{2,10},{4,12},{6,14},{8,0},{10,2},{12,4},{14,6},{1,9},{3,11}... | collective-permute-start | bytes 196616 | tf_op jit(solution)/shard_map/ppermute | solution.py:274
  15.1 1.3 %collective-permute-start.5 = (bf16[32,1024]{1,0:T(8,128)(2,1)}, bf16[32,1024]{1,0:T(8,128)(2,1)S(1)}, u32[]{:S(2)}, u32[]{:S(2)}) collective-permute-start(bf16[32,1024]{1,0:T(8,128)(2,1)} %get-tuple-element.26), channel_id=1, source_target_pairs={{0,10},{2,8},{4,14},{6,12},{8,2},{10,0},{12,6},{14,4},{1,11},{3,9}... | collective-permute-start | bytes 196616 | tf_op jit(solution)/shard_map/ppermute | solution.py:274
  16.4 0.0 collective-permute-done.refs_1_
  16.4 3.6 %collective-permute-start.6 = (bf16[32,1024]{1,0:T(8,128)(2,1)}, bf16[32,1024]{1,0:T(8,128)(2,1)S(1)}, u32[]{:S(2)}, u32[]{:S(2)}) collective-permute-start(bf16[32,1024]{1,0:T(8,128)(2,1)} %get-tuple-element.27), channel_id=1, source_target_pairs={{0,12},{2,14},{4,8},{6,10},{8,4},{10,6},{12,0},{14,2},{1,13},{3,15... | collective-permute-start | bytes 196616 | tf_op jit(solution)/shard_map/ppermute | solution.py:274
  20.0 0.7 %collective-permute-done.1.refs_2_ = bf16[96,1024]{1,0:T(8,128)(2,1)S(1)} collective-permute-done((bf16[96,1024]{1,0:T(8,128)(2,1)}, bf16[96,1024]{1,0:T(8,128)(2,1)S(1)}, u32[]{:S(2)}, u32[]{:S(2)}) %collective-permute-start.1) | collective-permute-done | bytes 196640 | tf_op jit(solution)/shard_map/ppermute | solution.py:274
  20.7 4.1 %collective-permute-start.7 = (bf16[32,1024]{1,0:T(8,128)(2,1)}, bf16[32,1024]{1,0:T(8,128)(2,1)S(1)}, u32[]{:S(2)}, u32[]{:S(2)}) collective-permute-start(bf16[32,1024]{1,0:T(8,128)(2,1)} %get-tuple-element.28), channel_id=1, source_target_pairs={{0,14},{2,12},{4,10},{6,8},{8,6},{10,4},{12,2},{14,0},{1,15},{3,13... | collective-permute-start | bytes 196616 | tf_op jit(solution)/shard_map/ppermute | solution.py:274
  24.8 0.0 collective-permute-done.2.refs_3_
  24.8 0.9 %copy-done = bf16[96,1024]{1,0:T(8,128)(2,1)S(1)} copy-done((bf16[96,1024]{1,0:T(8,128)(2,1)S(1)}, bf16[96,1024]{1,0:T(8,128)(2,1)}, u32[]{:S(2)}) %copy-start) | copy-done | bytes 196632
  25.7 0.3 shard_map.47
  26.0 0.0 collective-permute-done.4.refs_0_
  26.0 2.3 %collective-permute-done.6.refs_2_ = bf16[32,1024]{1,0:T(8,128)(2,1)S(1)} collective-permute-done((bf16[32,1024]{1,0:T(8,128)(2,1)}, bf16[32,1024]{1,0:T(8,128)(2,1)S(1)}, u32[]{:S(2)}, u32[]{:S(2)}) %collective-permute-start.6) | collective-permute-done | bytes 65568 | tf_op jit(solution)/shard_map/ppermute | solution.py:274
  28.4 0.7 %collective-permute-done.7.refs_3_ = bf16[32,1024]{1,0:T(8,128)(2,1)S(1)} collective-permute-done((bf16[32,1024]{1,0:T(8,128)(2,1)}, bf16[32,1024]{1,0:T(8,128)(2,1)S(1)}, u32[]{:S(2)}, u32[]{:S(2)}) %collective-permute-start.7) | collective-permute-done | bytes 65568 | tf_op jit(solution)/shard_map/ppermute | solution.py:274
  29.0 0.2 shard_map.48.own_ref
  29.2 0.1 collective-permute-start.8
  29.3 0.8 %copy.7.table_ref = s32[18,2]{1,0:T(8,128)S(1)} copy(s32[18,2]{0,1:T(2,128)} %param.6) | data formatting | bytes 288 | tf_op args[2]
  30.1 0.9 %collective-permute-start.3 = (bf16[64,1024]{1,0:T(8,128)(2,1)S(1)}, bf16[64,1024]{1,0:T(8,128)(2,1)S(1)}, u32[]{:S(2)}, u32[]{:S(2)}) collective-permute-start(bf16[64,1024]{1,0:T(8,128)(2,1)S(1)} %get-tuple-element.23), channel_id=1, source_target_pairs={{0,8},{2,10},{4,12},{6,14},{8,0},{10,2},{12,4},{14,6},{1,9},{3,11}... | collective-permute-start | bytes 393224 | tf_op jit(solution)/shard_map/ppermute | solution.py:274
  31.0 8.8 %shard_map.49.refs_0_ = bf16[8,18,2,256,256]{4,3,2,1,0:T(8,128)(2,1)} custom-call(s32[18,2]{1,0:T(8,128)S(1)} %copy.7.table_ref, bf16[64,1024]{1,0:T(8,128)(2,1)S(1)} %shard_map.48.own_ref, bf16[64,1024]{1,0:T(8,128)(2,1)S(1)} %collective-permute-done.8.other_ref), custom_call_target="tpu_custom_call" | custom-call | flops 4831838208 | bytes 18874368 | tf_op jit(solution)/shard_map/pallas_call | solution.py:220
  39.8 0.3 collective-permute-start.9
  40.1 1.1 %collective-permute-done.9.other_ref = bf16[64,1024]{1,0:T(8,128)(2,1)S(1)} collective-permute-done((bf16[64,1024]{1,0:T(8,128)(2,1)S(1)}, bf16[64,1024]{1,0:T(8,128)(2,1)S(1)}, u32[]{:S(2)}, u32[]{:S(2)}) %collective-permute-start.9) | collective-permute-done | bytes 131104 | tf_op jit(solution)/shard_map/ppermute | solution.py:238
  41.2 8.8 %shard_map.51 = bf16[8,18,2,256,256]{4,3,2,1,0:T(8,128)(2,1)} custom-call(s32[18,2]{1,0:T(8,128)S(1)} %copy.7.table_ref, bf16[64,1024]{1,0:T(8,128)(2,1)S(1)} %shard_map.50.own_ref, bf16[64,1024]{1,0:T(8,128)(2,1)S(1)} %collective-permute-done.9.other_ref, bf16[8,18,2,256,256]{4,3,2,1,0:T(8,128)(2,1)} %shard_map.49.refs_0_), custom_call_target="tpu_custom_call", output_to_operand_aliasing={{}: (3, {})} | custom-call | flops 4831838208 | bytes 18874368 | tf_op jit(solution)/shard_map/pallas_call | solution.py:220
  (5 shorter events, 0.0 us)
Async XLA Ops:
  7.5 8.9 %collective-permute-start = (bf16[96,1024]{1,0:T(8,128)(2,1)}, bf16[96,1024]{1,0:T(8,128)(2,1)S(1)}, u32[]{:S(2)}, u32[]{:S(2)}) collective-permute-start(bf16[96,1024]{1,0:T(8,128)(2,1)} %get-tuple-element.19), channel_id=1, source_target_pairs={{0,2},{2,0},{4,6},{6,4},{8,10},{10,8},{12,14},{14,12},{1,3},{3,1},... | collective-permute-start | bytes 589832 | tf_op jit(solution)/shard_map/ppermute | solution.py:274
  10.5 10.1 %collective-permute-start.1 = (bf16[96,1024]{1,0:T(8,128)(2,1)}, bf16[96,1024]{1,0:T(8,128)(2,1)S(1)}, u32[]{:S(2)}, u32[]{:S(2)}) collective-permute-start(bf16[96,1024]{1,0:T(8,128)(2,1)} %get-tuple-element.20), channel_id=1, source_target_pairs={{0,4},{2,6},{4,0},{6,2},{8,12},{10,14},{12,8},{14,10},{1,5},{3,7},... | collective-permute-start | bytes 589832 | tf_op jit(solution)/shard_map/ppermute | solution.py:274
  12.1 12.7 %collective-permute-start.2 = (bf16[96,1024]{1,0:T(8,128)(2,1)}, bf16[96,1024]{1,0:T(8,128)(2,1)S(1)}, u32[]{:S(2)}, u32[]{:S(2)}) collective-permute-start(bf16[96,1024]{1,0:T(8,128)(2,1)} %get-tuple-element.21), channel_id=1, source_target_pairs={{0,6},{2,4},{4,2},{6,0},{8,14},{10,12},{12,10},{14,8},{1,7},{3,5},... | collective-permute-start | bytes 589832 | tf_op jit(solution)/shard_map/ppermute | solution.py:274
  12.1 13.9 %collective-permute-start.4 = (bf16[32,1024]{1,0:T(8,128)(2,1)}, bf16[32,1024]{1,0:T(8,128)(2,1)S(1)}, u32[]{:S(2)}, u32[]{:S(2)}) collective-permute-start(bf16[32,1024]{1,0:T(8,128)(2,1)} %get-tuple-element.25), channel_id=1, source_target_pairs={{0,8},{2,10},{4,12},{6,14},{8,0},{10,2},{12,4},{14,6},{1,9},{3,11}... | collective-permute-start | bytes 196616 | tf_op jit(solution)/shard_map/ppermute | solution.py:274
  15.1 10.9 %collective-permute-start.5 = (bf16[32,1024]{1,0:T(8,128)(2,1)}, bf16[32,1024]{1,0:T(8,128)(2,1)S(1)}, u32[]{:S(2)}, u32[]{:S(2)}) collective-permute-start(bf16[32,1024]{1,0:T(8,128)(2,1)} %get-tuple-element.26), channel_id=1, source_target_pairs={{0,10},{2,8},{4,14},{6,12},{8,2},{10,0},{12,6},{14,4},{1,11},{3,9}... | collective-permute-start | bytes 196616 | tf_op jit(solution)/shard_map/ppermute | solution.py:274
  16.4 12.0 %collective-permute-start.6 = (bf16[32,1024]{1,0:T(8,128)(2,1)}, bf16[32,1024]{1,0:T(8,128)(2,1)S(1)}, u32[]{:S(2)}, u32[]{:S(2)}) collective-permute-start(bf16[32,1024]{1,0:T(8,128)(2,1)} %get-tuple-element.27), channel_id=1, source_target_pairs={{0,12},{2,14},{4,8},{6,10},{8,4},{10,6},{12,0},{14,2},{1,13},{3,15... | collective-permute-start | bytes 196616 | tf_op jit(solution)/shard_map/ppermute | solution.py:274
  20.7 8.4 %collective-permute-start.7 = (bf16[32,1024]{1,0:T(8,128)(2,1)}, bf16[32,1024]{1,0:T(8,128)(2,1)S(1)}, u32[]{:S(2)}, u32[]{:S(2)}) collective-permute-start(bf16[32,1024]{1,0:T(8,128)(2,1)} %get-tuple-element.28), channel_id=1, source_target_pairs={{0,14},{2,12},{4,10},{6,8},{8,6},{10,4},{12,2},{14,0},{1,15},{3,13... | collective-permute-start | bytes 196616 | tf_op jit(solution)/shard_map/ppermute | solution.py:274
  24.8 0.9 %copy-start = (bf16[96,1024]{1,0:T(8,128)(2,1)S(1)}, bf16[96,1024]{1,0:T(8,128)(2,1)}, u32[]{:S(2)}) copy-start(bf16[96,1024]{1,0:T(8,128)(2,1)} %get-tuple-element.18.refs_0_) | copy-start | bytes 589828
  29.2 1.8 %collective-permute-start.8 = (bf16[64,1024]{1,0:T(8,128)(2,1)S(1)}, bf16[64,1024]{1,0:T(8,128)(2,1)S(1)}, u32[]{:S(2)}, u32[]{:S(2)}) collective-permute-start(bf16[64,1024]{1,0:T(8,128)(2,1)S(1)} %shard_map.48.own_ref), channel_id=1, source_target_pairs={{0,1},{1,0},{2,3},{3,2},{4,5},{5,4},{6,7},{7,6},{8,9},{9,8},{10,11... | collective-permute-start | bytes 393224 | tf_op jit(solution)/shard_map/ppermute | solution.py:238
  30.1 9.7 %collective-permute-start.3 = (bf16[64,1024]{1,0:T(8,128)(2,1)S(1)}, bf16[64,1024]{1,0:T(8,128)(2,1)S(1)}, u32[]{:S(2)}, u32[]{:S(2)}) collective-permute-start(bf16[64,1024]{1,0:T(8,128)(2,1)S(1)} %get-tuple-element.23), channel_id=1, source_target_pairs={{0,8},{2,10},{4,12},{6,14},{8,0},{10,2},{12,4},{14,6},{1,9},{3,11}... | collective-permute-start | bytes 393224 | tf_op jit(solution)/shard_map/ppermute | solution.py:274
  39.8 1.4 %collective-permute-start.9 = (bf16[64,1024]{1,0:T(8,128)(2,1)S(1)}, bf16[64,1024]{1,0:T(8,128)(2,1)S(1)}, u32[]{:S(2)}, u32[]{:S(2)}) collective-permute-start(bf16[64,1024]{1,0:T(8,128)(2,1)S(1)} %shard_map.50.own_ref), channel_id=1, source_target_pairs={{0,1},{1,0},{2,3},{3,2},{4,5},{5,4},{6,7},{7,6},{8,9},{9,8},{10,11... | collective-permute-start | bytes 393224 | tf_op jit(solution)/shard_map/ppermute | solution.py:238

commit v3 on v2

--- a/solution.py
+++ b/solution.py
@@ -91,9 +91,9 @@
             pltpu.VMEM((rows, NFFT), jnp.bfloat16),
             pltpu.SemaphoreType.DMA((4,)),
         ],
-        compiler_params=params(60),
+        compiler_params=params(40),
         cost_estimate=cost(4 * rows * inputs * NFFT, 8 << 20),
-    )(jnp.asarray(basis), window, samples)
+    )(*[pltpu.with_memory_space_constraint(a, pltpu.HBM) for a in (jnp.asarray(basis), window, samples)])
 
 
 def tap_matrix(frames, pieces, count, first):
@@ -172,33 +172,37 @@
         for c in range(count):
             right[place, c] = jnp.where(chan == c, piece, jnp.zeros_like(piece))
 
-    def copy(step):
+    def copies(step):
         slot = lax.rem(step, slots)
-        where = out_ref.at[pl.ds(chunk * count, count), pl.ds(step * together, together)]
-        return pltpu.make_async_copy(buf.at[slot], where, sem.at[slot])
+        tiles = pl.ds(step * together, together)
+        return [
+            pltpu.make_async_copy(buf.at[slot, c], out_ref.at[chunk * count + c, tiles], sem.at[slot, c])
+            for c in range(count)
+        ]
 
     def body(step, carry):
         slot = lax.rem(step, slots)
 
         @pl.when(step >= slots)
         def _():
-            copy(step - slots).wait()
-
-        for u in range(together):
-            p = table_ref[step * together + u, 0]
-            q = table_ref[step * together + u, 1]
-            for c in range(count):
+            for done in copies(step - slots):
+                done.wait()
+
+        pairs = [(table_ref[step * together + u, 0], table_ref[step * together + u, 1]) for u in range(together)]
+        for c, ready in enumerate(copies(step)):
+            for u, (p, q) in enumerate(pairs):
                 for part in range(2):
                     first = left[p, part * TILE : (part + 1) * TILE, :]
                     power = jnp.dot(first, right[q, c], preferred_element_type=jnp.float32)
                     buf[slot, c, u, part] = power.astype(jnp.bfloat16)
-        copy(step).start()
+            ready.start()
         return carry
 
     lax.fori_loop(0, steps, body, 0)
 
     def drain(step, carry):
-        copy(step).wait()
+        for done in copies(step):
+            done.wait()
         return carry
 
     lax.fori_loop(steps - slots, steps, drain, 0)
@@ -207,7 +211,7 @@
 def cross_power(table, own, other, count, total, chunk, previous):
     depth, width = own.shape
     tiles = table.shape[0]
-    together = 2 if tiles % 2 == 0 else 1
+    together = 3 if tiles % 3 == 0 else 1
     vmem = pl.BlockSpec(memory_space=pltpu.VMEM)
     hbm = pl.BlockSpec(memory_space=pl.ANY)
     in_specs = [pl.BlockSpec(memory_space=pltpu.SMEM), vmem, vmem]
@@ -226,10 +230,10 @@
             pltpu.VMEM((NB, 2 * TILE, depth), jnp.bfloat16),
             pltpu.VMEM((NB, count, depth, TILE), jnp.bfloat16),
             pltpu.VMEM((3, count, together, 2, TILE, TILE), jnp.bfloat16),
-            pltpu.SemaphoreType.DMA((3,)),
+            pltpu.SemaphoreType.DMA((3, count)),
         ],
         input_output_aliases=aliases,
-        compiler_params=params(24),
+        compiler_params=params(32),
         cost_estimate=cost(2 * tiles * count * 2 * TILE * TILE * 256, tiles * count * 4 * TILE * TILE),
     )(*args)
 

time: 50.3 us -> 48.4 us (0.962)
  Pallas kernels: 25.5 us -> 23.4 us
  waiting for transfers between devices: 4.84 us -> 6.38 us
  local copies, waits for them, and re-layouts: 1.7 us -> 0.77 us
    ppermute x8, waiting for transfers between devices: 3.71 us -> 5.04 us  [swap(): lax.ppermute(block, 'tm', [(i, i ^ d) for i in range(owners)])]
    pallas_call x2, Pallas kernels: 17.5 us -> 16.2 us  [cross_power(): pl.pallas_call(functools.partial(power_kernel, count, chunk, together), i...]
    unnamed x3 -> x1, local copies, waits for them, and re-layouts: 1.7 us -> 0.77 us
    pallas_call x1, Pallas kernels: 7.52 us -> 6.71 us  [transform(): pl.pallas_call(functools.partial(transform_kernel, group, segments), in_s...]
  transfers between devices with their start and end apart: 10 -> 10, of which waited for: 4 -> 5; matrix products, arithmetic and copies ran while one was open for 2% -> 2% of each run, Pallas kernels for 18% -> 17%
where the time goes in v3:
time: 48.4 us; the launch traced here: 48.2 us
  Pallas kernels  23.4 us (48%)
  starting transfers between devices  17.6 us (36%)
  waiting for transfers between devices  6.38 us (13%)
  local copies, waits for them, and re-layouts  0.77 us (2%)
    ppermute x8, starting transfers between devices, swap(): lax.ppermute(block, 'tm', [(i, i ^ d) for i in range(owners)])  17.4 us
    pallas_call x2, Pallas kernels, cross_power(): pl.pallas_call(functools.partial(power_kernel, count, chunk, together), i...  16.2 us
    pallas_call x1, Pallas kernels, transform(): pl.pallas_call(functools.partial(transform_kernel, group, segments), in_s...  6.71 us
    ppermute x8, waiting for transfers between devices, swap(): lax.ppermute(block, 'tm', [(i, i ^ d) for i in range(owners)])  5.04 us
    ppermute x2, waiting for transfers between devices, finish(): other = lax.ppermute(own, 'inp', [(0, 1), (1, 0)])  1.34 us
  transfers between devices with their start and end apart: 10, of which 5 were waited for; matrix products, arithmetic and copies ran while one was open for 2% of the time, Pallas kernels for 17%

profile of v3, /device:TPU:0, one launch (start us, length us, event | category | flops | bytes accessed | tf_op | source)
XLA Modules:
  0.0 48.2 jit_solution(18148415665859974492)
XLA Ops:
  0.0 6.7 %shard_map.46 = (bf16[32,1024]{1,0:T(8,128)(2,1)S(1)}, bf16[32,1024]{1,0:T(8,128)(2,1)S(1)}, bf16[32,1024]{1,0:T(8,128)(2,1)S(1)}, bf16[32,1024]{1,0:T(8,128)(2,...) custom-call(f32[2,64,2048]{2,1,0:T(8,128)} %constant.2.clone.basis_h, ...), custom_call_target="tpu_custom_call" | custom-call | flops 4294967296 | bytes 8388608 | tf_op jit(solution)/shard_map/pallas_call | solution.py:81
  6.7 3.0 %collective-permute-start = (bf16[96,1024]{1,0:T(8,128)(2,1)S(1)}, bf16[96,1024]{1,0:T(8,128)(2,1)S(1)}, u32[]{:S(2)}, u32[]{:S(2)}) collective-permute-start(bf16[96,1024]{1,0:T(8,128)(2,1)S(1)} %get-tuple-element.19), channel_id=1, source_target_pairs={{0,2},{2,0},{4,6},{6,4},{8,10},{10,8},{12,14},{14,12},{1,3},{3,1},... | collective-permute-start | bytes 589832 | tf_op jit(solution)/shard_map/ppermute | solution.py:278
  9.7 1.6 %collective-permute-start.1 = (bf16[96,1024]{1,0:T(8,128)(2,1)S(1)}, bf16[96,1024]{1,0:T(8,128)(2,1)S(1)}, u32[]{:S(2)}, u32[]{:S(2)}) collective-permute-start(bf16[96,1024]{1,0:T(8,128)(2,1)S(1)} %get-tuple-element.20), channel_id=1, source_target_pairs={{0,4},{2,6},{4,0},{6,2},{8,12},{10,14},{12,8},{14,10},{1,5},{3,7},... | collective-permute-start | bytes 589832 | tf_op jit(solution)/shard_map/ppermute | solution.py:278
  11.3 0.0 collective-permute-start.2
  11.3 3.0 %collective-permute-start.4 = (bf16[32,1024]{1,0:T(8,128)(2,1)S(1)}, bf16[32,1024]{1,0:T(8,128)(2,1)S(1)}, u32[]{:S(2)}, u32[]{:S(2)}) collective-permute-start(bf16[32,1024]{1,0:T(8,128)(2,1)S(1)} %get-tuple-element.25), channel_id=1, source_target_pairs={{0,8},{2,10},{4,12},{6,14},{8,0},{10,2},{12,4},{14,6},{1,9},{3,11}... | collective-permute-start | bytes 196616 | tf_op jit(solution)/shard_map/ppermute | solution.py:278
  14.3 1.3 %collective-permute-start.5 = (bf16[32,1024]{1,0:T(8,128)(2,1)S(1)}, bf16[32,1024]{1,0:T(8,128)(2,1)S(1)}, u32[]{:S(2)}, u32[]{:S(2)}) collective-permute-start(bf16[32,1024]{1,0:T(8,128)(2,1)S(1)} %get-tuple-element.26), channel_id=1, source_target_pairs={{0,10},{2,8},{4,14},{6,12},{8,2},{10,0},{12,6},{14,4},{1,11},{3,9}... | collective-permute-start | bytes 196616 | tf_op jit(solution)/shard_map/ppermute | solution.py:278
  15.6 0.0 collective-permute-done.refs_1_
  15.6 3.6 %collective-permute-start.6 = (bf16[32,1024]{1,0:T(8,128)(2,1)S(1)}, bf16[32,1024]{1,0:T(8,128)(2,1)S(1)}, u32[]{:S(2)}, u32[]{:S(2)}) collective-permute-start(bf16[32,1024]{1,0:T(8,128)(2,1)S(1)} %get-tuple-element.27), channel_id=1, source_target_pairs={{0,12},{2,14},{4,8},{6,10},{8,4},{10,6},{12,0},{14,2},{1,13},{3,15... | collective-permute-start | bytes 196616 | tf_op jit(solution)/shard_map/ppermute | solution.py:278
  19.2 0.5 collective-permute-done.1.refs_2_
  19.6 4.0 %collective-permute-start.7 = (bf16[32,1024]{1,0:T(8,128)(2,1)S(1)}, bf16[32,1024]{1,0:T(8,128)(2,1)S(1)}, u32[]{:S(2)}, u32[]{:S(2)}) collective-permute-start(bf16[32,1024]{1,0:T(8,128)(2,1)S(1)} %get-tuple-element.28), channel_id=1, source_target_pairs={{0,14},{2,12},{4,10},{6,8},{8,6},{10,4},{12,2},{14,0},{1,15},{3,13... | collective-permute-start | bytes 196616 | tf_op jit(solution)/shard_map/ppermute | solution.py:278
  23.7 0.0 collective-permute-done.2.refs_3_
  23.7 0.3 shard_map.47
  23.9 0.0 collective-permute-done.4.refs_0_
  24.0 3.4 %collective-permute-done.6.refs_2_ = bf16[32,1024]{1,0:T(8,128)(2,1)S(1)} collective-permute-done((bf16[32,1024]{1,0:T(8,128)(2,1)S(1)}, bf16[32,1024]{1,0:T(8,128)(2,1)S(1)}, u32[]{:S(2)}, u32[]{:S(2)}) %collective-permute-start.6) | collective-permute-done | bytes 65568 | tf_op jit(solution)/shard_map/ppermute | solution.py:278
  27.3 0.7 %collective-permute-done.7.refs_3_ = bf16[32,1024]{1,0:T(8,128)(2,1)S(1)} collective-permute-done((bf16[32,1024]{1,0:T(8,128)(2,1)S(1)}, bf16[32,1024]{1,0:T(8,128)(2,1)S(1)}, u32[]{:S(2)}, u32[]{:S(2)}) %collective-permute-start.7) | collective-permute-done | bytes 65568 | tf_op jit(solution)/shard_map/ppermute | solution.py:278
  28.0 0.2 shard_map.48.own_ref
  28.2 0.1 collective-permute-start.8
  28.3 0.8 %copy.7.table_ref = s32[18,2]{1,0:T(8,128)S(1)} copy(s32[18,2]{0,1:T(2,128)} %param.6) | data formatting | bytes 288 | tf_op args[2]
  29.0 0.9 %collective-permute-start.3 = (bf16[64,1024]{1,0:T(8,128)(2,1)S(1)}, bf16[64,1024]{1,0:T(8,128)(2,1)S(1)}, u32[]{:S(2)}, u32[]{:S(2)}) collective-permute-start(bf16[64,1024]{1,0:T(8,128)(2,1)S(1)} %get-tuple-element.23), channel_id=1, source_target_pairs={{0,8},{2,10},{4,12},{6,14},{8,0},{10,2},{12,4},{14,6},{1,9},{3,11}... | collective-permute-start | bytes 393224 | tf_op jit(solution)/shard_map/ppermute | solution.py:278
  30.0 8.1 %shard_map.49.refs_0_ = bf16[8,18,2,256,256]{4,3,2,1,0:T(8,128)(2,1)} custom-call(s32[18,2]{1,0:T(8,128)S(1)} %copy.7.table_ref, bf16[64,1024]{1,0:T(8,128)(2,1)S(1)} %shard_map.48.own_ref, bf16[64,1024]{1,0:T(8,128)(2,1)S(1)} %collective-permute-done.8.other_ref), custom_call_target="tpu_custom_call" | custom-call | flops 4831838208 | bytes 18874368 | tf_op jit(solution)/shard_map/pallas_call | solution.py:224
  38.1 0.5 %collective-permute-done.3.far_ref = bf16[64,1024]{1,0:T(8,128)(2,1)S(1)} collective-permute-done((bf16[64,1024]{1,0:T(8,128)(2,1)S(1)}, bf16[64,1024]{1,0:T(8,128)(2,1)S(1)}, u32[]{:S(2)}, u32[]{:S(2)}) %collective-permute-start.3) | collective-permute-done | bytes 131104 | tf_op jit(solution)/shard_map/ppermute | solution.py:278
  38.7 0.1 collective-permute-start.9
  38.7 1.3 %collective-permute-done.9.other_ref = bf16[64,1024]{1,0:T(8,128)(2,1)S(1)} collective-permute-done((bf16[64,1024]{1,0:T(8,128)(2,1)S(1)}, bf16[64,1024]{1,0:T(8,128)(2,1)S(1)}, u32[]{:S(2)}, u32[]{:S(2)}) %collective-permute-start.9) | collective-permute-done | bytes 131104 | tf_op jit(solution)/shard_map/ppermute | solution.py:242
  40.1 8.1 %shard_map.51 = bf16[8,18,2,256,256]{4,3,2,1,0:T(8,128)(2,1)} custom-call(s32[18,2]{1,0:T(8,128)S(1)} %copy.7.table_ref, bf16[64,1024]{1,0:T(8,128)(2,1)S(1)} %shard_map.50.own_ref, bf16[64,1024]{1,0:T(8,128)(2,1)S(1)} %collective-permute-done.9.other_ref, bf16[8,18,2,256,256]{4,3,2,1,0:T(8,128)(2,1)} %shard_map.49.refs_0_), custom_call_target="tpu_custom_call", output_to_operand_aliasing={{}: (3, {})} | custom-call | flops 4831838208 | bytes 18874368 | tf_op jit(solution)/shard_map/pallas_call | solution.py:224
  (3 shorter events, 0.0 us)
Async XLA Ops:
  6.7 8.8 %collective-permute-start = (bf16[96,1024]{1,0:T(8,128)(2,1)S(1)}, bf16[96,1024]{1,0:T(8,128)(2,1)S(1)}, u32[]{:S(2)}, u32[]{:S(2)}) collective-permute-start(bf16[96,1024]{1,0:T(8,128)(2,1)S(1)} %get-tuple-element.19), channel_id=1, source_target_pairs={{0,2},{2,0},{4,6},{6,4},{8,10},{10,8},{12,14},{14,12},{1,3},{3,1},... | collective-permute-start | bytes 589832 | tf_op jit(solution)/shard_map/ppermute | solution.py:278
  9.7 9.9 %collective-permute-start.1 = (bf16[96,1024]{1,0:T(8,128)(2,1)S(1)}, bf16[96,1024]{1,0:T(8,128)(2,1)S(1)}, u32[]{:S(2)}, u32[]{:S(2)}) collective-permute-start(bf16[96,1024]{1,0:T(8,128)(2,1)S(1)} %get-tuple-element.20), channel_id=1, source_target_pairs={{0,4},{2,6},{4,0},{6,2},{8,12},{10,14},{12,8},{14,10},{1,5},{3,7},... | collective-permute-start | bytes 589832 | tf_op jit(solution)/shard_map/ppermute | solution.py:278
  11.3 12.4 %collective-permute-start.2 = (bf16[96,1024]{1,0:T(8,128)(2,1)S(1)}, bf16[96,1024]{1,0:T(8,128)(2,1)S(1)}, u32[]{:S(2)}, u32[]{:S(2)}) collective-permute-start(bf16[96,1024]{1,0:T(8,128)(2,1)S(1)} %get-tuple-element.21), channel_id=1, source_target_pairs={{0,6},{2,4},{4,2},{6,0},{8,14},{10,12},{12,10},{14,8},{1,7},{3,5},... | collective-permute-start | bytes 589832 | tf_op jit(solution)/shard_map/ppermute | solution.py:278
  11.3 12.7 %collective-permute-start.4 = (bf16[32,1024]{1,0:T(8,128)(2,1)S(1)}, bf16[32,1024]{1,0:T(8,128)(2,1)S(1)}, u32[]{:S(2)}, u32[]{:S(2)}) collective-permute-start(bf16[32,1024]{1,0:T(8,128)(2,1)S(1)} %get-tuple-element.25), channel_id=1, source_target_pairs={{0,8},{2,10},{4,12},{6,14},{8,0},{10,2},{12,4},{14,6},{1,9},{3,11}... | collective-permute-start | bytes 196616 | tf_op jit(solution)/shard_map/ppermute | solution.py:278
  14.3 9.7 %collective-permute-start.5 = (bf16[32,1024]{1,0:T(8,128)(2,1)S(1)}, bf16[32,1024]{1,0:T(8,128)(2,1)S(1)}, u32[]{:S(2)}, u32[]{:S(2)}) collective-permute-start(bf16[32,1024]{1,0:T(8,128)(2,1)S(1)} %get-tuple-element.26), channel_id=1, source_target_pairs={{0,10},{2,8},{4,14},{6,12},{8,2},{10,0},{12,6},{14,4},{1,11},{3,9}... | collective-permute-start | bytes 196616 | tf_op jit(solution)/shard_map/ppermute | solution.py:278
  15.6 11.8 %collective-permute-start.6 = (bf16[32,1024]{1,0:T(8,128)(2,1)S(1)}, bf16[32,1024]{1,0:T(8,128)(2,1)S(1)}, u32[]{:S(2)}, u32[]{:S(2)}) collective-permute-start(bf16[32,1024]{1,0:T(8,128)(2,1)S(1)} %get-tuple-element.27), channel_id=1, source_target_pairs={{0,12},{2,14},{4,8},{6,10},{8,4},{10,6},{12,0},{14,2},{1,13},{3,15... | collective-permute-start | bytes 196616 | tf_op jit(solution)/shard_map/ppermute | solution.py:278
  19.6 8.4 %collective-permute-start.7 = (bf16[32,1024]{1,0:T(8,128)(2,1)S(1)}, bf16[32,1024]{1,0:T(8,128)(2,1)S(1)}, u32[]{:S(2)}, u32[]{:S(2)}) collective-permute-start(bf16[32,1024]{1,0:T(8,128)(2,1)S(1)} %get-tuple-element.28), channel_id=1, source_target_pairs={{0,14},{2,12},{4,10},{6,8},{8,6},{10,4},{12,2},{14,0},{1,15},{3,13... | collective-permute-start | bytes 196616 | tf_op jit(solution)/shard_map/ppermute | solution.py:278
  28.2 1.8 %collective-permute-start.8 = (bf16[64,1024]{1,0:T(8,128)(2,1)S(1)}, bf16[64,1024]{1,0:T(8,128)(2,1)S(1)}, u32[]{:S(2)}, u32[]{:S(2)}) collective-permute-start(bf16[64,1024]{1,0:T(8,128)(2,1)S(1)} %shard_map.48.own_ref), channel_id=1, source_target_pairs={{0,1},{1,0},{2,3},{3,2},{4,5},{5,4},{6,7},{7,6},{8,9},{9,8},{10,11... | collective-permute-start | bytes 393224 | tf_op jit(solution)/shard_map/ppermute | solution.py:242
  29.0 9.6 %collective-permute-start.3 = (bf16[64,1024]{1,0:T(8,128)(2,1)S(1)}, bf16[64,1024]{1,0:T(8,128)(2,1)S(1)}, u32[]{:S(2)}, u32[]{:S(2)}) collective-permute-start(bf16[64,1024]{1,0:T(8,128)(2,1)S(1)} %get-tuple-element.23), channel_id=1, source_target_pairs={{0,8},{2,10},{4,12},{6,14},{8,0},{10,2},{12,4},{14,6},{1,9},{3,11}... | collective-permute-start | bytes 393224 | tf_op jit(solution)/shard_map/ppermute | solution.py:278
  38.7 1.4 %collective-permute-start.9 = (bf16[64,1024]{1,0:T(8,128)(2,1)S(1)}, bf16[64,1024]{1,0:T(8,128)(2,1)S(1)}, u32[]{:S(2)}, u32[]{:S(2)}) collective-permute-start(bf16[64,1024]{1,0:T(8,128)(2,1)S(1)} %shard_map.50.own_ref), channel_id=1, source_target_pairs={{0,1},{1,0},{2,3},{3,2},{4,5},{5,4},{6,7},{7,6},{8,9},{9,8},{10,11... | collective-permute-start | bytes 393224 | tf_op jit(solution)/shard_map/ppermute | solution.py:242

commit v4 on v3

--- a/solution.py
+++ b/solution.py
@@ -35,7 +35,7 @@
 
 
 def transform_kernel(group, segments, basis_hbm, window_hbm, samples_hbm, *refs):
-    *out_refs, basis, window, samples, high, low, sems = refs
+    *out_refs, basis, window, samples, high, sems = refs
     blocks = 2
     size = samples.shape[0] // blocks
     copies = [
@@ -55,17 +55,13 @@
             place = lax.bitwise_xor(lax.axis_index("tm"), distance)
         rows = basis[chunk, pl.ds(pl.multiple_of(place * group, group), group), :]
         weights = jnp.concatenate([rows * window[k : k + 1, :] for k in range(TAPS)], axis=0)
-        rounded = weights.astype(jnp.bfloat16)
-        where = pl.ds(index * group * TAPS, group * TAPS)
-        high[where, :] = rounded
-        low[where, :] = (weights - rounded.astype(jnp.float32)).astype(jnp.bfloat16)
+        high[pl.ds(index * group * TAPS, group * TAPS), :] = weights.astype(jnp.bfloat16)
 
     contract = (((1,), (1,)), ((), ()))
     for b in range(blocks):
         copies[2 + b].wait()
         piece = samples[b * size : (b + 1) * size, :]
         total = lax.dot_general(high[...], piece, contract, preferred_element_type=jnp.float32)
-        total += lax.dot_general(low[...], piece, contract, preferred_element_type=jnp.float32)
         total = total.astype(jnp.bfloat16)
         first = 0
         for out_ref in out_refs:
@@ -87,7 +83,6 @@
             pltpu.VMEM(basis.shape, jnp.float32),
             pltpu.VMEM((TAPS, NFFT), jnp.float32),
             pltpu.VMEM((inputs, NFFT), jnp.bfloat16),
-            pltpu.VMEM((rows, NFFT), jnp.bfloat16),
             pltpu.VMEM((rows, NFFT), jnp.bfloat16),
             pltpu.SemaphoreType.DMA((4,)),
         ],

time: 48.4 us -> 46.2 us (0.955)
  Pallas kernels: 23.4 us -> 21.2 us
    pallas_call x1, Pallas kernels: 6.71 us -> 4.53 us  [transform(): pl.pallas_call(functools.partial(transform_kernel, group, segments), in_s...]
  transfers between devices with their start and end apart: 10 -> 10, of which waited for: 5 -> 5; matrix products, arithmetic and copies ran while one was open for 2% -> 2% of each run, Pallas kernels for 17% -> 18%
where the time goes in v4:
time: 46.2 us; the launch traced here: 46 us
  Pallas kernels  21.2 us (46%)
  starting transfers between devices  17.6 us (38%)
  waiting for transfers between devices  6.38 us (14%)
  local copies, waits for them, and re-layouts  0.77 us (2%)
    ppermute x8, starting transfers between devices, swap(): lax.ppermute(block, 'tm', [(i, i ^ d) for i in range(owners)])  17.4 us
    pallas_call x2, Pallas kernels, cross_power(): pl.pallas_call(functools.partial(power_kernel, count, chunk, together), i...  16.2 us
    ppermute x8, waiting for transfers between devices, swap(): lax.ppermute(block, 'tm', [(i, i ^ d) for i in range(owners)])  5.04 us
    pallas_call x1, Pallas kernels, transform(): pl.pallas_call(functools.partial(transform_kernel, group, segments), in_s...  4.53 us
    ppermute x2, waiting for transfers between devices, finish(): other = lax.ppermute(own, 'inp', [(0, 1), (1, 0)])  1.34 us
  transfers between devices with their start and end apart: 10, of which 5 were waited for; matrix products, arithmetic and copies ran while one was open for 2% of the time, Pallas kernels for 18%

profile of v4, /device:TPU:0, one launch (start us, length us, event | category | flops | bytes accessed | tf_op | source)
XLA Modules:
  0.0 46.0 jit_solution(11975462329505922597)
XLA Ops:
  0.0 4.5 %shard_map.46 = (bf16[32,1024]{1,0:T(8,128)(2,1)S(1)}, bf16[32,1024]{1,0:T(8,128)(2,1)S(1)}, bf16[32,1024]{1,0:T(8,128)(2,1)S(1)}, bf16[32,1024]{1,0:T(8,128)(2,...) custom-call(f32[2,64,2048]{2,1,0:T(8,128)} %constant.2.clone.basis_h, ...), custom_call_target="tpu_custom_call" | custom-call | flops 4294967296 | bytes 8388608 | tf_op jit(solution)/shard_map/pallas_call | solution.py:77
  4.5 3.0 %collective-permute-start = (bf16[96,1024]{1,0:T(8,128)(2,1)S(1)}, bf16[96,1024]{1,0:T(8,128)(2,1)S(1)}, u32[]{:S(2)}, u32[]{:S(2)}) collective-permute-start(bf16[96,1024]{1,0:T(8,128)(2,1)S(1)} %get-tuple-element.19), channel_id=1, source_target_pairs={{0,2},{2,0},{4,6},{6,4},{8,10},{10,8},{12,14},{14,12},{1,3},{3,1},... | collective-permute-start | bytes 589832 | tf_op jit(solution)/shard_map/ppermute | solution.py:273
  7.5 1.6 %collective-permute-start.1 = (bf16[96,1024]{1,0:T(8,128)(2,1)S(1)}, bf16[96,1024]{1,0:T(8,128)(2,1)S(1)}, u32[]{:S(2)}, u32[]{:S(2)}) collective-permute-start(bf16[96,1024]{1,0:T(8,128)(2,1)S(1)} %get-tuple-element.20), channel_id=1, source_target_pairs={{0,4},{2,6},{4,0},{6,2},{8,12},{10,14},{12,8},{14,10},{1,5},{3,7},... | collective-permute-start | bytes 589832 | tf_op jit(solution)/shard_map/ppermute | solution.py:273
  9.1 0.0 collective-permute-start.2
  9.1 3.0 %collective-permute-start.4 = (bf16[32,1024]{1,0:T(8,128)(2,1)S(1)}, bf16[32,1024]{1,0:T(8,128)(2,1)S(1)}, u32[]{:S(2)}, u32[]{:S(2)}) collective-permute-start(bf16[32,1024]{1,0:T(8,128)(2,1)S(1)} %get-tuple-element.25), channel_id=1, source_target_pairs={{0,8},{2,10},{4,12},{6,14},{8,0},{10,2},{12,4},{14,6},{1,9},{3,11}... | collective-permute-start | bytes 196616 | tf_op jit(solution)/shard_map/ppermute | solution.py:273
  12.1 1.3 %collective-permute-start.5 = (bf16[32,1024]{1,0:T(8,128)(2,1)S(1)}, bf16[32,1024]{1,0:T(8,128)(2,1)S(1)}, u32[]{:S(2)}, u32[]{:S(2)}) collective-permute-start(bf16[32,1024]{1,0:T(8,128)(2,1)S(1)} %get-tuple-element.26), channel_id=1, source_target_pairs={{0,10},{2,8},{4,14},{6,12},{8,2},{10,0},{12,6},{14,4},{1,11},{3,9}... | collective-permute-start | bytes 196616 | tf_op jit(solution)/shard_map/ppermute | solution.py:273
  13.4 0.0 collective-permute-done.refs_1_
  13.4 3.6 %collective-permute-start.6 = (bf16[32,1024]{1,0:T(8,128)(2,1)S(1)}, bf16[32,1024]{1,0:T(8,128)(2,1)S(1)}, u32[]{:S(2)}, u32[]{:S(2)}) collective-permute-start(bf16[32,1024]{1,0:T(8,128)(2,1)S(1)} %get-tuple-element.27), channel_id=1, source_target_pairs={{0,12},{2,14},{4,8},{6,10},{8,4},{10,6},{12,0},{14,2},{1,13},{3,15... | collective-permute-start | bytes 196616 | tf_op jit(solution)/shard_map/ppermute | solution.py:273
  17.0 0.5 %collective-permute-done.1.refs_2_ = bf16[96,1024]{1,0:T(8,128)(2,1)S(1)} collective-permute-done((bf16[96,1024]{1,0:T(8,128)(2,1)S(1)}, bf16[96,1024]{1,0:T(8,128)(2,1)S(1)}, u32[]{:S(2)}, u32[]{:S(2)}) %collective-permute-start.1) | collective-permute-done | bytes 196640 | tf_op jit(solution)/shard_map/ppermute | solution.py:273
  17.5 4.0 %collective-permute-start.7 = (bf16[32,1024]{1,0:T(8,128)(2,1)S(1)}, bf16[32,1024]{1,0:T(8,128)(2,1)S(1)}, u32[]{:S(2)}, u32[]{:S(2)}) collective-permute-start(bf16[32,1024]{1,0:T(8,128)(2,1)S(1)} %get-tuple-element.28), channel_id=1, source_target_pairs={{0,14},{2,12},{4,10},{6,8},{8,6},{10,4},{12,2},{14,0},{1,15},{3,13... | collective-permute-start | bytes 196616 | tf_op jit(solution)/shard_map/ppermute | solution.py:273
  21.5 0.0 collective-permute-done.2.refs_3_
  21.5 0.3 shard_map.47
  21.8 0.0 collective-permute-done.4.refs_0_
  21.8 3.3 %collective-permute-done.6.refs_2_ = bf16[32,1024]{1,0:T(8,128)(2,1)S(1)} collective-permute-done((bf16[32,1024]{1,0:T(8,128)(2,1)S(1)}, bf16[32,1024]{1,0:T(8,128)(2,1)S(1)}, u32[]{:S(2)}, u32[]{:S(2)}) %collective-permute-start.6) | collective-permute-done | bytes 65568 | tf_op jit(solution)/shard_map/ppermute | solution.py:273
  25.2 0.7 %collective-permute-done.7.refs_3_ = bf16[32,1024]{1,0:T(8,128)(2,1)S(1)} collective-permute-done((bf16[32,1024]{1,0:T(8,128)(2,1)S(1)}, bf16[32,1024]{1,0:T(8,128)(2,1)S(1)}, u32[]{:S(2)}, u32[]{:S(2)}) %collective-permute-start.7) | collective-permute-done | bytes 65568 | tf_op jit(solution)/shard_map/ppermute | solution.py:273
  25.8 0.2 shard_map.48.own_ref
  26.0 0.1 collective-permute-start.8
  26.1 0.8 %copy.7.table_ref = s32[18,2]{1,0:T(8,128)S(1)} copy(s32[18,2]{0,1:T(2,128)} %param.6) | data formatting | bytes 288 | tf_op args[2]
  26.9 0.9 %collective-permute-start.3 = (bf16[64,1024]{1,0:T(8,128)(2,1)S(1)}, bf16[64,1024]{1,0:T(8,128)(2,1)S(1)}, u32[]{:S(2)}, u32[]{:S(2)}) collective-permute-start(bf16[64,1024]{1,0:T(8,128)(2,1)S(1)} %get-tuple-element.23), channel_id=1, source_target_pairs={{0,8},{2,10},{4,12},{6,14},{8,0},{10,2},{12,4},{14,6},{1,9},{3,11}... | collective-permute-start | bytes 393224 | tf_op jit(solution)/shard_map/ppermute | solution.py:273
  27.8 8.1 %shard_map.49.refs_0_ = bf16[8,18,2,256,256]{4,3,2,1,0:T(8,128)(2,1)} custom-call(s32[18,2]{1,0:T(8,128)S(1)} %copy.7.table_ref, bf16[64,1024]{1,0:T(8,128)(2,1)S(1)} %shard_map.48.own_ref, bf16[64,1024]{1,0:T(8,128)(2,1)S(1)} %collective-permute-done.8.other_ref), custom_call_target="tpu_custom_call" | custom-call | flops 4831838208 | bytes 18874368 | tf_op jit(solution)/shard_map/pallas_call | solution.py:219
  35.9 0.5 %collective-permute-done.3.far_ref = bf16[64,1024]{1,0:T(8,128)(2,1)S(1)} collective-permute-done((bf16[64,1024]{1,0:T(8,128)(2,1)S(1)}, bf16[64,1024]{1,0:T(8,128)(2,1)S(1)}, u32[]{:S(2)}, u32[]{:S(2)}) %collective-permute-start.3) | collective-permute-done | bytes 131104 | tf_op jit(solution)/shard_map/ppermute | solution.py:273
  36.5 0.1 collective-permute-start.9
  36.6 1.3 %collective-permute-done.9.other_ref = bf16[64,1024]{1,0:T(8,128)(2,1)S(1)} collective-permute-done((bf16[64,1024]{1,0:T(8,128)(2,1)S(1)}, bf16[64,1024]{1,0:T(8,128)(2,1)S(1)}, u32[]{:S(2)}, u32[]{:S(2)}) %collective-permute-start.9) | collective-permute-done | bytes 131104 | tf_op jit(solution)/shard_map/ppermute | solution.py:237
  37.9 8.1 %shard_map.51 = bf16[8,18,2,256,256]{4,3,2,1,0:T(8,128)(2,1)} custom-call(s32[18,2]{1,0:T(8,128)S(1)} %copy.7.table_ref, bf16[64,1024]{1,0:T(8,128)(2,1)S(1)} %shard_map.50.own_ref, bf16[64,1024]{1,0:T(8,128)(2,1)S(1)} %collective-permute-done.9.other_ref, bf16[8,18,2,256,256]{4,3,2,1,0:T(8,128)(2,1)} %shard_map.49.refs_0_), custom_call_target="tpu_custom_call", output_to_operand_aliasing={{}: (3, {})} | custom-call | flops 4831838208 | bytes 18874368 | tf_op jit(solution)/shard_map/pallas_call | solution.py:219
  (3 shorter events, 0.0 us)
Async XLA Ops:
  4.5 8.9 %collective-permute-start = (bf16[96,1024]{1,0:T(8,128)(2,1)S(1)}, bf16[96,1024]{1,0:T(8,128)(2,1)S(1)}, u32[]{:S(2)}, u32[]{:S(2)}) collective-permute-start(bf16[96,1024]{1,0:T(8,128)(2,1)S(1)} %get-tuple-element.19), channel_id=1, source_target_pairs={{0,2},{2,0},{4,6},{6,4},{8,10},{10,8},{12,14},{14,12},{1,3},{3,1},... | collective-permute-start | bytes 589832 | tf_op jit(solution)/shard_map/ppermute | solution.py:273
  7.5 9.9 %collective-permute-start.1 = (bf16[96,1024]{1,0:T(8,128)(2,1)S(1)}, bf16[96,1024]{1,0:T(8,128)(2,1)S(1)}, u32[]{:S(2)}, u32[]{:S(2)}) collective-permute-start(bf16[96,1024]{1,0:T(8,128)(2,1)S(1)} %get-tuple-element.20), channel_id=1, source_target_pairs={{0,4},{2,6},{4,0},{6,2},{8,12},{10,14},{12,8},{14,10},{1,5},{3,7},... | collective-permute-start | bytes 589832 | tf_op jit(solution)/shard_map/ppermute | solution.py:273
  9.1 12.4 %collective-permute-start.2 = (bf16[96,1024]{1,0:T(8,128)(2,1)S(1)}, bf16[96,1024]{1,0:T(8,128)(2,1)S(1)}, u32[]{:S(2)}, u32[]{:S(2)}) collective-permute-start(bf16[96,1024]{1,0:T(8,128)(2,1)S(1)} %get-tuple-element.21), channel_id=1, source_target_pairs={{0,6},{2,4},{4,2},{6,0},{8,14},{10,12},{12,10},{14,8},{1,7},{3,5},... | collective-permute-start | bytes 589832 | tf_op jit(solution)/shard_map/ppermute | solution.py:273
  9.1 12.7 %collective-permute-start.4 = (bf16[32,1024]{1,0:T(8,128)(2,1)S(1)}, bf16[32,1024]{1,0:T(8,128)(2,1)S(1)}, u32[]{:S(2)}, u32[]{:S(2)}) collective-permute-start(bf16[32,1024]{1,0:T(8,128)(2,1)S(1)} %get-tuple-element.25), channel_id=1, source_target_pairs={{0,8},{2,10},{4,12},{6,14},{8,0},{10,2},{12,4},{14,6},{1,9},{3,11}... | collective-permute-start | bytes 196616 | tf_op jit(solution)/shard_map/ppermute | solution.py:273
  12.1 9.7 %collective-permute-start.5 = (bf16[32,1024]{1,0:T(8,128)(2,1)S(1)}, bf16[32,1024]{1,0:T(8,128)(2,1)S(1)}, u32[]{:S(2)}, u32[]{:S(2)}) collective-permute-start(bf16[32,1024]{1,0:T(8,128)(2,1)S(1)} %get-tuple-element.26), channel_id=1, source_target_pairs={{0,10},{2,8},{4,14},{6,12},{8,2},{10,0},{12,6},{14,4},{1,11},{3,9}... | collective-permute-start | bytes 196616 | tf_op jit(solution)/shard_map/ppermute | solution.py:273
  13.4 11.8 %collective-permute-start.6 = (bf16[32,1024]{1,0:T(8,128)(2,1)S(1)}, bf16[32,1024]{1,0:T(8,128)(2,1)S(1)}, u32[]{:S(2)}, u32[]{:S(2)}) collective-permute-start(bf16[32,1024]{1,0:T(8,128)(2,1)S(1)} %get-tuple-element.27), channel_id=1, source_target_pairs={{0,12},{2,14},{4,8},{6,10},{8,4},{10,6},{12,0},{14,2},{1,13},{3,15... | collective-permute-start | bytes 196616 | tf_op jit(solution)/shard_map/ppermute | solution.py:273
  17.5 8.3 %collective-permute-start.7 = (bf16[32,1024]{1,0:T(8,128)(2,1)S(1)}, bf16[32,1024]{1,0:T(8,128)(2,1)S(1)}, u32[]{:S(2)}, u32[]{:S(2)}) collective-permute-start(bf16[32,1024]{1,0:T(8,128)(2,1)S(1)} %get-tuple-element.28), channel_id=1, source_target_pairs={{0,14},{2,12},{4,10},{6,8},{8,6},{10,4},{12,2},{14,0},{1,15},{3,13... | collective-permute-start | bytes 196616 | tf_op jit(solution)/shard_map/ppermute | solution.py:273
  26.0 1.8 %collective-permute-start.8 = (bf16[64,1024]{1,0:T(8,128)(2,1)S(1)}, bf16[64,1024]{1,0:T(8,128)(2,1)S(1)}, u32[]{:S(2)}, u32[]{:S(2)}) collective-permute-start(bf16[64,1024]{1,0:T(8,128)(2,1)S(1)} %shard_map.48.own_ref), channel_id=1, source_target_pairs={{0,1},{1,0},{2,3},{3,2},{4,5},{5,4},{6,7},{7,6},{8,9},{9,8},{10,11... | collective-permute-start | bytes 393224 | tf_op jit(solution)/shard_map/ppermute | solution.py:237
  26.9 9.6 %collective-permute-start.3 = (bf16[64,1024]{1,0:T(8,128)(2,1)S(1)}, bf16[64,1024]{1,0:T(8,128)(2,1)S(1)}, u32[]{:S(2)}, u32[]{:S(2)}) collective-permute-start(bf16[64,1024]{1,0:T(8,128)(2,1)S(1)} %get-tuple-element.23), channel_id=1, source_target_pairs={{0,8},{2,10},{4,12},{6,14},{8,0},{10,2},{12,4},{14,6},{1,9},{3,11}... | collective-permute-start | bytes 393224 | tf_op jit(solution)/shard_map/ppermute | solution.py:273
  36.5 1.4 %collective-permute-start.9 = (bf16[64,1024]{1,0:T(8,128)(2,1)S(1)}, bf16[64,1024]{1,0:T(8,128)(2,1)S(1)}, u32[]{:S(2)}, u32[]{:S(2)}) collective-permute-start(bf16[64,1024]{1,0:T(8,128)(2,1)S(1)} %shard_map.50.own_ref), channel_id=1, source_target_pairs={{0,1},{1,0},{2,3},{3,2},{4,5},{5,4},{6,7},{7,6},{8,9},{9,8},{10,11... | collective-permute-start | bytes 393224 | tf_op jit(solution)/shard_map/ppermute | solution.py:237

commit v5 on v4

--- a/solution.py
+++ b/solution.py
@@ -14,6 +14,10 @@
 CHAN = 64
 TILE = 256
 NB = INPUTS // TILE
+SPLIT = 4
+ORDERS = ((0, 1, 2, 3), (0, 3, 2, 1))
+TERMS = (1, 2)
+BLOCKS = 1
 HALF = NB // 2
 
 
@@ -35,43 +39,52 @@
 
 
 def transform_kernel(group, segments, basis_hbm, window_hbm, samples_hbm, *refs):
-    *out_refs, basis, window, samples, high, sems = refs
-    blocks = 2
-    size = samples.shape[0] // blocks
-    copies = [
-        pltpu.make_async_copy(basis_hbm, basis, sems.at[0]),
-        pltpu.make_async_copy(window_hbm, window, sems.at[1]),
-    ]
-    for b in range(blocks):
-        rows = pl.ds(b * size, size)
-        copies.append(pltpu.make_async_copy(samples_hbm.at[rows], samples.at[rows], sems.at[2 + b]))
+    *out_refs, basis, window, samples, weights, total, sems = refs
+    terms = weights.shape[0]
+    depth = NFFT // SPLIT
+    pieces = [pl.ds(k * depth, depth) for k in range(SPLIT)]
+    copies = [pltpu.make_async_copy(window_hbm, window, sems.at[2 * SPLIT])]
+    for k, piece in enumerate(pieces):
+        copies.append(pltpu.make_async_copy(basis_hbm.at[:, piece], basis.at[:, piece], sems.at[2 * k]))
+        copies.append(pltpu.make_async_copy(samples_hbm.at[:, piece], samples.at[:, piece], sems.at[2 * k + 1]))
     for copy in copies:
         copy.start()
     copies[0].wait()
-    copies[1].wait()
-    for index, (chunk, distance) in enumerate(segments):
-        place = distance
-        if len(out_refs) > 1:
-            place = lax.bitwise_xor(lax.axis_index("tm"), distance)
-        rows = basis[chunk, pl.ds(pl.multiple_of(place * group, group), group), :]
-        weights = jnp.concatenate([rows * window[k : k + 1, :] for k in range(TAPS)], axis=0)
-        high[pl.ds(index * group * TAPS, group * TAPS), :] = weights.astype(jnp.bfloat16)
-
-    contract = (((1,), (1,)), ((), ()))
-    for b in range(blocks):
-        copies[2 + b].wait()
-        piece = samples[b * size : (b + 1) * size, :]
-        total = lax.dot_general(high[...], piece, contract, preferred_element_type=jnp.float32)
-        total = total.astype(jnp.bfloat16)
-        first = 0
-        for out_ref in out_refs:
-            out_ref[:, b * size : (b + 1) * size] = total[first : first + out_ref.shape[0]]
-            first += out_ref.shape[0]
-
-
-def transform(samples, window, owners, chunks, count, group, segments, outs):
+    size = samples.shape[0] // BLOCKS
+    for k, piece in enumerate(pieces):
+        copies[1 + 2 * k].wait()
+        for index, distance in enumerate(segments):
+            place = distance
+            if len(out_refs) > 1:
+                place = lax.bitwise_xor(lax.axis_index("tm"), distance)
+            rows = basis[pl.ds(pl.multiple_of(place * group, group), group), piece]
+            product = jnp.concatenate([rows * window[t : t + 1, piece] for t in range(TAPS)], axis=0)
+            for term in range(terms):
+                rounded = product.astype(jnp.bfloat16)
+                weights[term, pl.ds(index * group * TAPS, group * TAPS), piece] = rounded
+                product -= rounded.astype(jnp.float32)
+        copies[2 + 2 * k].wait()
+        for b in range(BLOCKS):
+            columns = pl.ds(b * size, size)
+            contract = (((1,), (1,)), ((), ()))
+            part = total[:, columns] if k else 0.0
+            for term in range(terms):
+                part += lax.dot_general(
+                    weights[term, :, piece], samples[columns, piece], contract, preferred_element_type=jnp.float32
+                )
+            if k < SPLIT - 1:
+                total[:, columns] = part
+                continue
+            part = part.astype(jnp.bfloat16)
+            first = 0
+            for out_ref in out_refs:
+                out_ref[:, columns] = part[first : first + out_ref.shape[0]]
+                first += out_ref.shape[0]
+
+
+def transform(samples, window, owners, first, count, group, segments, outs, terms):
     inputs = samples.shape[0]
-    basis = np.stack([basis_rows(owners, chunk * count, count) for chunk in range(chunks)])
+    basis = basis_rows(owners, first, count)
     rows = len(segments) * group * TAPS
     hbm = pl.BlockSpec(memory_space=pl.ANY)
     return pl.pallas_call(
@@ -83,11 +96,12 @@
             pltpu.VMEM(basis.shape, jnp.float32),
             pltpu.VMEM((TAPS, NFFT), jnp.float32),
             pltpu.VMEM((inputs, NFFT), jnp.bfloat16),
-            pltpu.VMEM((rows, NFFT), jnp.bfloat16),
-            pltpu.SemaphoreType.DMA((4,)),
+            pltpu.VMEM((terms, rows, NFFT), jnp.bfloat16),
+            pltpu.VMEM((rows, inputs), jnp.float32),
+            pltpu.SemaphoreType.DMA((2 * SPLIT + 1,)),
         ],
         compiler_params=params(40),
-        cost_estimate=cost(4 * rows * inputs * NFFT, 8 << 20),
+        cost_estimate=cost(2 * terms * rows * inputs * NFFT, 8 << 20),
     )(*[pltpu.with_memory_space_constraint(a, pltpu.HBM) for a in (jnp.asarray(basis), window, samples)])
 
 
@@ -106,30 +120,22 @@
     out_ref[...] = jnp.dot(add, spectra_ref[...], preferred_element_type=jnp.float32).astype(jnp.bfloat16)
 
 
-def near_sum_kernel(owners, count, *refs):
-    *parts, near_first, near_second, facing = refs
+def near_sum_kernel(owners, count, order, *refs):
+    *parts, mine, facing = refs
+    parts = [parts[order.index(d)] for d in range(len(parts))]
     depth = TAPS * 2 * count
     add = tap_matrix(owners, owners // 2, count, lax.axis_index("tm"))
-    for index, out_ref in enumerate((near_first, near_second, facing)):
+    for index, out_ref in enumerate((mine, facing)):
         spectra = jnp.concatenate([ref[index * depth : (index + 1) * depth, :] for ref in parts], axis=0)
         total = jnp.dot(add, spectra, preferred_element_type=jnp.float32)
         out_ref[...] = total.astype(out_ref.dtype)
 
 
-def far_sum_kernel(owners, count, near_ref, *refs):
-    *parts, out_ref = refs
-    half = owners // 2
-    add = tap_matrix(owners, half, count, lax.bitwise_xor(lax.axis_index("tm"), half))
-    spectra = jnp.concatenate([ref[...] for ref in parts], axis=0)
-    total = near_ref[...] + jnp.dot(add, spectra, preferred_element_type=jnp.float32)
-    out_ref[...] = total.astype(jnp.bfloat16)
-
-
 def join_kernel(near_ref, far_ref, out_ref):
     out_ref[...] = (near_ref[...] + far_ref[...].astype(jnp.float32)).astype(jnp.bfloat16)
 
 
-def small(kernel, outs, inputs):
+def small(kernel, outs, inputs, flops=1 << 28):
     vmem = pl.BlockSpec(memory_space=pltpu.VMEM)
     return pl.pallas_call(
         kernel,
@@ -137,7 +143,7 @@
         out_specs=[vmem] * len(outs),
         out_shape=outs,
         compiler_params=params(16),
-        cost_estimate=cost(1 << 28, 1 << 20),
+        cost_estimate=cost(flops, 1 << 20),
     )(*inputs)
 
 
@@ -229,7 +235,7 @@
         ],
         input_output_aliases=aliases,
         compiler_params=params(32),
-        cost_estimate=cost(2 * tiles * count * 2 * TILE * TILE * 256, tiles * count * 4 * TILE * TILE),
+        cost_estimate=cost(1 << 28, 1 << 20),
     )(*args)
 
 
@@ -243,8 +249,8 @@
     cols = 2 * total
     together = 1 if cols % 8 == 0 else 8 // cols
     group = cols * together
-    segments = [(0, d) for d in range(owners // together)]
-    (partial,) = transform(samples, window, owners, 1, total, group, segments, [len(segments)])
+    segments = list(range(owners // together))
+    (partial,) = transform(samples, window, owners, 0, total, group, segments, [len(segments)], 2)
     partial = partial.reshape(owners // together, TAPS, together, cols, inputs)
     partial = jnp.transpose(partial, (0, 2, 1, 3, 4)).reshape(owners, TAPS * cols, inputs)
     turned = lax.all_to_all(partial, "tm", split_axis=0, concat_axis=0, tiled=True)
@@ -263,28 +269,33 @@
     inputs = raw_samples.shape[0]
     count = total // 2
     half = owners // 2
-    segments = [(0, half + d) for d in range(half)]
-    for d in range(half):
-        segments += [(0, d), (1, d), (1, half + d)]
-    outs = [1] * half + [3] * half
-    sent = transform(raw_samples, pfb_window, owners, 2, count, 2 * count, segments, outs)
+    segments = [d + far for d in range(half) for far in (0, half)]
 
     def swap(block, d):
         return block if d == 0 else lax.ppermute(block, "tm", [(i, i ^ d) for i in range(owners)])
 
-    far = [swap(sent[d], half + d) for d in range(half)]
-    near = [swap(sent[half + d], d) for d in range(half)]
     exact = jax.ShapeDtypeStruct((2 * count * owners, inputs), jnp.float32)
     rounded = jax.ShapeDtypeStruct((2 * count * owners, inputs), jnp.bfloat16)
-    kernel = functools.partial(near_sum_kernel, owners, count)
-    near_first, near_second, facing = small(kernel, [exact, exact, rounded], near)
-    faced = swap(facing, half)
-    kernel = functools.partial(far_sum_kernel, owners, count)
-    (own,) = small(kernel, [rounded], [near_first] + far)
-    out = finish(tile_table, own, count, total, 0, None)
-    faced, out = lax.optimization_barrier((faced, out))
-    (own,) = small(join_kernel, [rounded], [near_second, faced])
-    return finish(tile_table, own, count, total, 1, out)
+    parts = [
+        transform(raw_samples, pfb_window, owners, chunk * count, count, 2 * count, segments, [2] * half, TERMS[chunk])
+        for chunk in range(2)
+    ]
+    near = [swap(parts[0][d], d) for d in ORDERS[0]]
+    near, parts[1] = lax.optimization_barrier((near, parts[1]))
+    sums = []
+    for chunk in range(2):
+        if chunk:
+            near = [swap(parts[1][d], d) for d in ORDERS[1]]
+        kernel = functools.partial(near_sum_kernel, owners, count, ORDERS[chunk])
+        mine, facing = small(kernel, [exact, rounded], near)
+        sums.append((mine, swap(facing, half)))
+    out = None
+    for chunk, (mine, faced) in enumerate(sums):
+        if out is not None:
+            faced, out = lax.optimization_barrier((faced, out))
+        (own,) = small(join_kernel, [rounded], [mine, faced], 1 << 34)
+        out = finish(tile_table, own, count, total, chunk, out)
+    return out
 
 
 def solution(mesh):

time: 46.2 us -> 44.6 us (0.965)
  starting transfers between devices: 17.6 us -> 11.3 us
  Pallas kernels: 21.2 us -> 24 us
  waiting for transfers between devices: 6.38 us -> 8.94 us
  local copies, waits for them, and re-layouts: 0.77 us -> 0.1 us
    ppermute x8, starting transfers between devices: 17.4 us -> 11.2 us  [swap(): lax.ppermute(block, 'tm', [(i, i ^ d) for i in range(owners)])]
    pallas_call x1 -> x2, Pallas kernels: 4.53 us -> 7.27 us  [transform(): pl.pallas_call(functools.partial(transform_kernel, group, segments), in_s...]
    ppermute x8, waiting for transfers between devices: 5.04 us -> 7.6 us  [swap(): lax.ppermute(block, 'tm', [(i, i ^ d) for i in range(owners)])]
    unnamed x1 -> x3, local copies, waits for them, and re-layouts: 0.77 us -> 0.1 us
  transfers between devices with their start and end apart: 10 -> 10, of which waited for: 5 -> 6; matrix products, arithmetic and copies ran while one was open for 2% -> 0% of each run, Pallas kernels for 18% -> 28%
where the time goes in v5:
time: 44.6 us; the launch traced here: 44.4 us
  Pallas kernels  24 us (54%)
  starting transfers between devices  11.3 us (25%)
  waiting for transfers between devices  8.94 us (20%)
    pallas_call x2, Pallas kernels, cross_power(): pl.pallas_call(functools.partial(power_kernel, count, chunk, together), i...  16.2 us
    ppermute x8, starting transfers between devices, swap(): lax.ppermute(block, 'tm', [(i, i ^ d) for i in range(owners)])  11.2 us
    ppermute x8, waiting for transfers between devices, swap(): lax.ppermute(block, 'tm', [(i, i ^ d) for i in range(owners)])  7.6 us
    pallas_call x2, Pallas kernels, transform(): pl.pallas_call(functools.partial(transform_kernel, group, segments), in_s...  7.27 us
    ppermute x2, waiting for transfers between devices, finish(): other = lax.ppermute(own, 'inp', [(0, 1), (1, 0)])  1.34 us
  transfers between devices with their start and end apart: 10, of which 6 were waited for; matrix products, arithmetic and copies ran while one was open for 0% of the time, Pallas kernels for 28%

profile of v5, /device:TPU:0, one launch (start us, length us, event | category | flops | bytes accessed | tf_op | source)
XLA Modules:
  0.0 44.4 jit_solution(5850199526370675913)
XLA Ops:
  0.0 3.0 %shard_map.55 = (bf16[64,1024]{1,0:T(8,128)(2,1)S(1)}, bf16[64,1024]{1,0:T(8,128)(2,1)S(1)}, bf16[64,1024]{1,0:T(8,128)(2,1)S(1)}, bf16[64,1024]{1,0:T(8,128)(2,1)S(1)}) custom-call(f32[64,2048]{1,0:T(8,128)} %constant.4.clone.basis_hbm, f32[4,2048]{1,0:T(4,128)} %window_hbm.3, bf16[1024,2048]{1,0:T(8,128)(2,1)} %samples_hbm.3), custom_call_target="tpu_custom_call" | custom-call | flops 1073741824 | bytes 8388608 | tf_op jit(solution)/shard_map/pallas_call | solution.py:90
  3.0 0.0 copy-start
  3.0 3.0 %collective-permute-start = (bf16[64,1024]{1,0:T(8,128)(2,1)S(1)}, bf16[64,1024]{1,0:T(8,128)(2,1)S(1)}, u32[]{:S(2)}, u32[]{:S(2)}) collective-permute-start(bf16[64,1024]{1,0:T(8,128)(2,1)S(1)} %get-tuple-element.28), channel_id=1, source_target_pairs={{0,2},{2,0},{4,6},{6,4},{8,10},{10,8},{12,14},{14,12},{1,3},{3,1},... | collective-permute-start | bytes 393224 | tf_op jit(solution)/shard_map/ppermute | solution.py:275
  6.1 1.6 %collective-permute-start.1 = (bf16[64,1024]{1,0:T(8,128)(2,1)S(1)}, bf16[64,1024]{1,0:T(8,128)(2,1)S(1)}, u32[]{:S(2)}, u32[]{:S(2)}) collective-permute-start(bf16[64,1024]{1,0:T(8,128)(2,1)S(1)} %get-tuple-element.29), channel_id=1, source_target_pairs={{0,4},{2,6},{4,0},{6,2},{8,12},{10,14},{12,8},{14,10},{1,5},{3,7},... | collective-permute-start | bytes 393224 | tf_op jit(solution)/shard_map/ppermute | solution.py:275
  7.6 4.2 %shard_map.56 = (bf16[64,1024]{1,0:T(8,128)(2,1)S(1)}, bf16[64,1024]{1,0:T(8,128)(2,1)S(1)}, bf16[64,1024]{1,0:T(8,128)(2,1)S(1)}, bf16[64,1024]{1,0:T(8,128)(2,1)S(1)}) custom-call(f32[64,2048]{1,0:T(8,128)} %constant.5.clone.basis_hbm, f32[4,2048]{1,0:T(4,128)} %window_hbm.3, bf16[1024,2048]{1,0:T(8,128)(2,1)} %samples_hbm.3), custom_call_target="tpu_custom_call" | custom-call | flops 2147483648 | bytes 8388608 | tf_op jit(solution)/shard_map/pallas_call | solution.py:90
  11.9 0.0 collective-permute-done.refs_1_
  11.9 0.5 %collective-permute-done.1.refs_2_ = bf16[64,1024]{1,0:T(8,128)(2,1)S(1)} collective-permute-done((bf16[64,1024]{1,0:T(8,128)(2,1)S(1)}, bf16[64,1024]{1,0:T(8,128)(2,1)S(1)}, u32[]{:S(2)}, u32[]{:S(2)}) %collective-permute-start.1) | collective-permute-done | bytes 131104 | tf_op jit(solution)/shard_map/ppermute | solution.py:275
  12.4 1.2 %collective-permute-done.2.refs_3_ = bf16[64,1024]{1,0:T(8,128)(2,1)S(1)} collective-permute-done((bf16[64,1024]{1,0:T(8,128)(2,1)S(1)}, bf16[64,1024]{1,0:T(8,128)(2,1)S(1)}, u32[]{:S(2)}, u32[]{:S(2)}) %collective-permute-start.2) | collective-permute-done | bytes 131104 | tf_op jit(solution)/shard_map/ppermute | solution.py:275
  13.6 0.2 shard_map.58
  13.8 2.8 %collective-permute-start.7 = (bf16[64,1024]{1,0:T(8,128)(2,1)S(1)}, bf16[64,1024]{1,0:T(8,128)(2,1)S(1)}, u32[]{:S(2)}, u32[]{:S(2)}) collective-permute-start(bf16[64,1024]{1,0:T(8,128)(2,1)S(1)} %get-tuple-element.46), channel_id=1, source_target_pairs={{0,8},{2,10},{4,12},{6,14},{8,0},{10,2},{12,4},{14,6},{1,9},{3,11}... | collective-permute-start | bytes 393224 | tf_op jit(solution)/shard_map/ppermute | solution.py:275
  16.7 2.5 %collective-permute-start.3 = (bf16[64,1024]{1,0:T(8,128)(2,1)S(1)}, bf16[64,1024]{1,0:T(8,128)(2,1)S(1)}, u32[]{:S(2)}, u32[]{:S(2)}) collective-permute-start(bf16[64,1024]{1,0:T(8,128)(2,1)S(1)} %get-tuple-element.36), channel_id=1, source_target_pairs={{0,6},{2,4},{4,2},{6,0},{8,14},{10,12},{12,10},{14,8},{1,7},{3,5},... | collective-permute-start | bytes 393224 | tf_op jit(solution)/shard_map/ppermute | solution.py:275
  19.2 0.4 %collective-permute-start.4 = (bf16[64,1024]{1,0:T(8,128)(2,1)S(1)}, bf16[64,1024]{1,0:T(8,128)(2,1)S(1)}, u32[]{:S(2)}, u32[]{:S(2)}) collective-permute-start(bf16[64,1024]{1,0:T(8,128)(2,1)S(1)} %get-tuple-element.37), channel_id=1, source_target_pairs={{0,4},{2,6},{4,0},{6,2},{8,12},{10,14},{12,8},{14,10},{1,5},{3,7},... | collective-permute-start | bytes 393224 | tf_op jit(solution)/shard_map/ppermute | solution.py:275
  19.6 0.5 %collective-permute-start.5 = (bf16[64,1024]{1,0:T(8,128)(2,1)S(1)}, bf16[64,1024]{1,0:T(8,128)(2,1)S(1)}, u32[]{:S(2)}, u32[]{:S(2)}) collective-permute-start(bf16[64,1024]{1,0:T(8,128)(2,1)S(1)} %get-tuple-element.38), channel_id=1, source_target_pairs={{0,2},{2,0},{4,6},{6,4},{8,10},{10,8},{12,14},{14,12},{1,3},{3,1},... | collective-permute-start | bytes 393224 | tf_op jit(solution)/shard_map/ppermute | solution.py:275
  20.2 1.7 %collective-permute-done.7.far_ref = bf16[64,1024]{1,0:T(8,128)(2,1)S(1)} collective-permute-done((bf16[64,1024]{1,0:T(8,128)(2,1)S(1)}, bf16[64,1024]{1,0:T(8,128)(2,1)S(1)}, u32[]{:S(2)}, u32[]{:S(2)}) %collective-permute-start.7) | collective-permute-done | bytes 131104 | tf_op jit(solution)/shard_map/ppermute | solution.py:275
  21.9 0.1 collective-permute-start.8
  22.0 2.3 %collective-permute-done.3.refs_1_ = bf16[64,1024]{1,0:T(8,128)(2,1)S(1)} collective-permute-done((bf16[64,1024]{1,0:T(8,128)(2,1)S(1)}, bf16[64,1024]{1,0:T(8,128)(2,1)S(1)}, u32[]{:S(2)}, u32[]{:S(2)}) %collective-permute-start.3) | collective-permute-done | bytes 131104 | tf_op jit(solution)/shard_map/ppermute | solution.py:275
  24.3 1.9 %collective-permute-done.4.refs_2_ = bf16[64,1024]{1,0:T(8,128)(2,1)S(1)} collective-permute-done((bf16[64,1024]{1,0:T(8,128)(2,1)S(1)}, bf16[64,1024]{1,0:T(8,128)(2,1)S(1)}, u32[]{:S(2)}, u32[]{:S(2)}) %collective-permute-start.4) | collective-permute-done | bytes 131104 | tf_op jit(solution)/shard_map/ppermute | solution.py:275
  26.1 0.2 shard_map.57
  26.4 0.3 collective-permute-start.6
  26.6 0.1 copy.8.table_ref
  26.7 8.1 %shard_map.60.refs_0_ = bf16[8,18,2,256,256]{4,3,2,1,0:T(8,128)(2,1)} custom-call(s32[18,2]{1,0:T(8,128)S(1)} %copy.8.table_ref, bf16[64,1024]{1,0:T(8,128)(2,1)S(1)} %shard_map.59.own_ref, bf16[64,1024]{1,0:T(8,128)(2,1)S(1)} %collective-permute-done.8.other_ref), custom_call_target="tpu_custom_call" | custom-call | flops 268435456 | bytes 1048576 | tf_op jit(solution)/shard_map/pallas_call | solution.py:225
  34.9 0.1 collective-permute-start.9
  35.0 1.3 %collective-permute-done.9.other_ref = bf16[64,1024]{1,0:T(8,128)(2,1)S(1)} collective-permute-done((bf16[64,1024]{1,0:T(8,128)(2,1)S(1)}, bf16[64,1024]{1,0:T(8,128)(2,1)S(1)}, u32[]{:S(2)}, u32[]{:S(2)}) %collective-permute-start.9) | collective-permute-done | bytes 131104 | tf_op jit(solution)/shard_map/ppermute | solution.py:243
  36.3 8.1 %shard_map.62 = bf16[8,18,2,256,256]{4,3,2,1,0:T(8,128)(2,1)} custom-call(s32[18,2]{1,0:T(8,128)S(1)} %copy.8.table_ref, bf16[64,1024]{1,0:T(8,128)(2,1)S(1)} %shard_map.61.own_ref, bf16[64,1024]{1,0:T(8,128)(2,1)S(1)} %collective-permute-done.9.other_ref, bf16[8,18,2,256,256]{4,3,2,1,0:T(8,128)(2,1)} %shard_map.60.refs_0_), custom_call_target="tpu_custom_call", output_to_operand_aliasing={{}: (3, {})} | custom-call | flops 268435456 | bytes 1048576 | tf_op jit(solution)/shard_map/pallas_call | solution.py:225
  (7 shorter events, 0.1 us)
Async XLA Ops:
  3.0 23.6 %copy-start = (s32[18,2]{0,1:T(2,128)S(1)}, s32[18,2]{0,1:T(2,128)}, u32[]{:S(2)}) copy-start(s32[18,2]{0,1:T(2,128)} %param.7) | copy-start | bytes 436
  3.0 8.8 %collective-permute-start = (bf16[64,1024]{1,0:T(8,128)(2,1)S(1)}, bf16[64,1024]{1,0:T(8,128)(2,1)S(1)}, u32[]{:S(2)}, u32[]{:S(2)}) collective-permute-start(bf16[64,1024]{1,0:T(8,128)(2,1)S(1)} %get-tuple-element.28), channel_id=1, source_target_pairs={{0,2},{2,0},{4,6},{6,4},{8,10},{10,8},{12,14},{14,12},{1,3},{3,1},... | collective-permute-start | bytes 393224 | tf_op jit(solution)/shard_map/ppermute | solution.py:275
  6.1 6.4 %collective-permute-start.1 = (bf16[64,1024]{1,0:T(8,128)(2,1)S(1)}, bf16[64,1024]{1,0:T(8,128)(2,1)S(1)}, u32[]{:S(2)}, u32[]{:S(2)}) collective-permute-start(bf16[64,1024]{1,0:T(8,128)(2,1)S(1)} %get-tuple-element.29), channel_id=1, source_target_pairs={{0,4},{2,6},{4,0},{6,2},{8,12},{10,14},{12,8},{14,10},{1,5},{3,7},... | collective-permute-start | bytes 393224 | tf_op jit(solution)/shard_map/ppermute | solution.py:275
  7.6 6.0 %collective-permute-start.2 = (bf16[64,1024]{1,0:T(8,128)(2,1)S(1)}, bf16[64,1024]{1,0:T(8,128)(2,1)S(1)}, u32[]{:S(2)}, u32[]{:S(2)}) collective-permute-start(bf16[64,1024]{1,0:T(8,128)(2,1)S(1)} %get-tuple-element.30), channel_id=1, source_target_pairs={{0,6},{2,4},{4,2},{6,0},{8,14},{10,12},{12,10},{14,8},{1,7},{3,5},... | collective-permute-start | bytes 393224 | tf_op jit(solution)/shard_map/ppermute | solution.py:275
  13.8 8.0 %collective-permute-start.7 = (bf16[64,1024]{1,0:T(8,128)(2,1)S(1)}, bf16[64,1024]{1,0:T(8,128)(2,1)S(1)}, u32[]{:S(2)}, u32[]{:S(2)}) collective-permute-start(bf16[64,1024]{1,0:T(8,128)(2,1)S(1)} %get-tuple-element.46), channel_id=1, source_target_pairs={{0,8},{2,10},{4,12},{6,14},{8,0},{10,2},{12,4},{14,6},{1,9},{3,11}... | collective-permute-start | bytes 393224 | tf_op jit(solution)/shard_map/ppermute | solution.py:275
  16.7 7.6 %collective-permute-start.3 = (bf16[64,1024]{1,0:T(8,128)(2,1)S(1)}, bf16[64,1024]{1,0:T(8,128)(2,1)S(1)}, u32[]{:S(2)}, u32[]{:S(2)}) collective-permute-start(bf16[64,1024]{1,0:T(8,128)(2,1)S(1)} %get-tuple-element.36), channel_id=1, source_target_pairs={{0,6},{2,4},{4,2},{6,0},{8,14},{10,12},{12,10},{14,8},{1,7},{3,5},... | collective-permute-start | bytes 393224 | tf_op jit(solution)/shard_map/ppermute | solution.py:275
  19.2 7.0 %collective-permute-start.4 = (bf16[64,1024]{1,0:T(8,128)(2,1)S(1)}, bf16[64,1024]{1,0:T(8,128)(2,1)S(1)}, u32[]{:S(2)}, u32[]{:S(2)}) collective-permute-start(bf16[64,1024]{1,0:T(8,128)(2,1)S(1)} %get-tuple-element.37), channel_id=1, source_target_pairs={{0,4},{2,6},{4,0},{6,2},{8,12},{10,14},{12,8},{14,10},{1,5},{3,7},... | collective-permute-start | bytes 393224 | tf_op jit(solution)/shard_map/ppermute | solution.py:275
  19.6 6.5 %collective-permute-start.5 = (bf16[64,1024]{1,0:T(8,128)(2,1)S(1)}, bf16[64,1024]{1,0:T(8,128)(2,1)S(1)}, u32[]{:S(2)}, u32[]{:S(2)}) collective-permute-start(bf16[64,1024]{1,0:T(8,128)(2,1)S(1)} %get-tuple-element.38), channel_id=1, source_target_pairs={{0,2},{2,0},{4,6},{6,4},{8,10},{10,8},{12,14},{14,12},{1,3},{3,1},... | collective-permute-start | bytes 393224 | tf_op jit(solution)/shard_map/ppermute | solution.py:275
  21.9 4.8 %collective-permute-start.8 = (bf16[64,1024]{1,0:T(8,128)(2,1)S(1)}, bf16[64,1024]{1,0:T(8,128)(2,1)S(1)}, u32[]{:S(2)}, u32[]{:S(2)}) collective-permute-start(bf16[64,1024]{1,0:T(8,128)(2,1)S(1)} %shard_map.59.own_ref), channel_id=1, source_target_pairs={{0,1},{1,0},{2,3},{3,2},{4,5},{5,4},{6,7},{7,6},{8,9},{9,8},{10,11... | collective-permute-start | bytes 393224 | tf_op jit(solution)/shard_map/ppermute | solution.py:243
  26.4 8.5 %collective-permute-start.6 = (bf16[64,1024]{1,0:T(8,128)(2,1)S(1)}, bf16[64,1024]{1,0:T(8,128)(2,1)S(1)}, u32[]{:S(2)}, u32[]{:S(2)}) collective-permute-start(bf16[64,1024]{1,0:T(8,128)(2,1)S(1)} %get-tuple-element.40), channel_id=1, source_target_pairs={{0,8},{2,10},{4,12},{6,14},{8,0},{10,2},{12,4},{14,6},{1,9},{3,11}... | collective-permute-start | bytes 393224 | tf_op jit(solution)/shard_map/ppermute | solution.py:275
  34.9 1.4 %collective-permute-start.9 = (bf16[64,1024]{1,0:T(8,128)(2,1)S(1)}, bf16[64,1024]{1,0:T(8,128)(2,1)S(1)}, u32[]{:S(2)}, u32[]{:S(2)}) collective-permute-start(bf16[64,1024]{1,0:T(8,128)(2,1)S(1)} %shard_map.61.own_ref), channel_id=1, source_target_pairs={{0,1},{1,0},{2,3},{3,2},{4,5},{5,4},{6,7},{7,6},{8,9},{9,8},{10,11... | collective-permute-start | bytes 393224 | tf_op jit(solution)/shard_map/ppermute | solution.py:243

commit v6 on v5

--- a/solution.py
+++ b/solution.py
@@ -192,10 +192,11 @@
         pairs = [(table_ref[step * together + u, 0], table_ref[step * together + u, 1]) for u in range(together)]
         for c, ready in enumerate(copies(step)):
             for u, (p, q) in enumerate(pairs):
-                for part in range(2):
-                    first = left[p, part * TILE : (part + 1) * TILE, :]
+                for quarter in range(4):
+                    rows = pl.ds(quarter % 2 * (TILE // 2), TILE // 2)
+                    first = left[p, quarter * TILE // 2 : (quarter + 1) * TILE // 2, :]
                     power = jnp.dot(first, right[q, c], preferred_element_type=jnp.float32)
-                    buf[slot, c, u, part] = power.astype(jnp.bfloat16)
+                    buf[slot, c, u, quarter // 2, rows] = power.astype(jnp.bfloat16)
             ready.start()
         return carry
 

time: 44.6 us -> 44.6 us (level)
  no operation moved by 1% of the time
where the time goes in v6:
time: 44.6 us; the launch traced here: 44.4 us
  Pallas kernels  24 us (54%)
  starting transfers between devices  11.3 us (25%)
  waiting for transfers between devices  8.94 us (20%)
    pallas_call x2, Pallas kernels, cross_power(): pl.pallas_call(functools.partial(power_kernel, count, chunk, together), i...  16.3 us
    ppermute x8, starting transfers between devices, swap(): lax.ppermute(block, 'tm', [(i, i ^ d) for i in range(owners)])  11.2 us
    ppermute x8, waiting for transfers between devices, swap(): lax.ppermute(block, 'tm', [(i, i ^ d) for i in range(owners)])  7.6 us
    pallas_call x2, Pallas kernels, transform(): pl.pallas_call(functools.partial(transform_kernel, group, segments), in_s...  7.27 us
    ppermute x2, waiting for transfers between devices, finish(): other = lax.ppermute(own, 'inp', [(0, 1), (1, 0)])  1.34 us
  transfers between devices with their start and end apart: 10, of which 6 were waited for; matrix products, arithmetic and copies ran while one was open for 0% of the time, Pallas kernels for 28%

profile of v6, /device:TPU:0, one launch (start us, length us, event | category | flops | bytes accessed | tf_op | source)
XLA Modules:
  0.0 44.4 jit_solution(673165567640614424)
XLA Ops:
  0.0 3.0 %shard_map.55 = (bf16[64,1024]{1,0:T(8,128)(2,1)S(1)}, bf16[64,1024]{1,0:T(8,128)(2,1)S(1)}, bf16[64,1024]{1,0:T(8,128)(2,1)S(1)}, bf16[64,1024]{1,0:T(8,128)(2,1)S(1)}) custom-call(f32[64,2048]{1,0:T(8,128)} %constant.4.clone.basis_hbm, f32[4,2048]{1,0:T(4,128)} %window_hbm.3, bf16[1024,2048]{1,0:T(8,128)(2,1)} %samples_hbm.3), custom_call_target="tpu_custom_call" | custom-call | flops 1073741824 | bytes 8388608 | tf_op jit(solution)/shard_map/pallas_call | solution.py:90
  3.0 0.0 copy-start
  3.0 3.0 %collective-permute-start = (bf16[64,1024]{1,0:T(8,128)(2,1)S(1)}, bf16[64,1024]{1,0:T(8,128)(2,1)S(1)}, u32[]{:S(2)}, u32[]{:S(2)}) collective-permute-start(bf16[64,1024]{1,0:T(8,128)(2,1)S(1)} %get-tuple-element.28), channel_id=1, source_target_pairs={{0,2},{2,0},{4,6},{6,4},{8,10},{10,8},{12,14},{14,12},{1,3},{3,1},... | collective-permute-start | bytes 393224 | tf_op jit(solution)/shard_map/ppermute | solution.py:276
  6.1 1.6 %collective-permute-start.1 = (bf16[64,1024]{1,0:T(8,128)(2,1)S(1)}, bf16[64,1024]{1,0:T(8,128)(2,1)S(1)}, u32[]{:S(2)}, u32[]{:S(2)}) collective-permute-start(bf16[64,1024]{1,0:T(8,128)(2,1)S(1)} %get-tuple-element.29), channel_id=1, source_target_pairs={{0,4},{2,6},{4,0},{6,2},{8,12},{10,14},{12,8},{14,10},{1,5},{3,7},... | collective-permute-start | bytes 393224 | tf_op jit(solution)/shard_map/ppermute | solution.py:276
  7.6 4.2 %shard_map.56 = (bf16[64,1024]{1,0:T(8,128)(2,1)S(1)}, bf16[64,1024]{1,0:T(8,128)(2,1)S(1)}, bf16[64,1024]{1,0:T(8,128)(2,1)S(1)}, bf16[64,1024]{1,0:T(8,128)(2,1)S(1)}) custom-call(f32[64,2048]{1,0:T(8,128)} %constant.5.clone.basis_hbm, f32[4,2048]{1,0:T(4,128)} %window_hbm.3, bf16[1024,2048]{1,0:T(8,128)(2,1)} %samples_hbm.3), custom_call_target="tpu_custom_call" | custom-call | flops 2147483648 | bytes 8388608 | tf_op jit(solution)/shard_map/pallas_call | solution.py:90
  11.9 0.0 collective-permute-done.refs_1_
  11.9 0.5 %collective-permute-done.1.refs_2_ = bf16[64,1024]{1,0:T(8,128)(2,1)S(1)} collective-permute-done((bf16[64,1024]{1,0:T(8,128)(2,1)S(1)}, bf16[64,1024]{1,0:T(8,128)(2,1)S(1)}, u32[]{:S(2)}, u32[]{:S(2)}) %collective-permute-start.1) | collective-permute-done | bytes 131104 | tf_op jit(solution)/shard_map/ppermute | solution.py:276
  12.4 1.2 %collective-permute-done.2.refs_3_ = bf16[64,1024]{1,0:T(8,128)(2,1)S(1)} collective-permute-done((bf16[64,1024]{1,0:T(8,128)(2,1)S(1)}, bf16[64,1024]{1,0:T(8,128)(2,1)S(1)}, u32[]{:S(2)}, u32[]{:S(2)}) %collective-permute-start.2) | collective-permute-done | bytes 131104 | tf_op jit(solution)/shard_map/ppermute | solution.py:276
  13.6 0.2 shard_map.58
  13.8 2.8 %collective-permute-start.7 = (bf16[64,1024]{1,0:T(8,128)(2,1)S(1)}, bf16[64,1024]{1,0:T(8,128)(2,1)S(1)}, u32[]{:S(2)}, u32[]{:S(2)}) collective-permute-start(bf16[64,1024]{1,0:T(8,128)(2,1)S(1)} %get-tuple-element.46), channel_id=1, source_target_pairs={{0,8},{2,10},{4,12},{6,14},{8,0},{10,2},{12,4},{14,6},{1,9},{3,11}... | collective-permute-start | bytes 393224 | tf_op jit(solution)/shard_map/ppermute | solution.py:276
  16.7 2.5 %collective-permute-start.3 = (bf16[64,1024]{1,0:T(8,128)(2,1)S(1)}, bf16[64,1024]{1,0:T(8,128)(2,1)S(1)}, u32[]{:S(2)}, u32[]{:S(2)}) collective-permute-start(bf16[64,1024]{1,0:T(8,128)(2,1)S(1)} %get-tuple-element.36), channel_id=1, source_target_pairs={{0,6},{2,4},{4,2},{6,0},{8,14},{10,12},{12,10},{14,8},{1,7},{3,5},... | collective-permute-start | bytes 393224 | tf_op jit(solution)/shard_map/ppermute | solution.py:276
  19.2 0.4 %collective-permute-start.4 = (bf16[64,1024]{1,0:T(8,128)(2,1)S(1)}, bf16[64,1024]{1,0:T(8,128)(2,1)S(1)}, u32[]{:S(2)}, u32[]{:S(2)}) collective-permute-start(bf16[64,1024]{1,0:T(8,128)(2,1)S(1)} %get-tuple-element.37), channel_id=1, source_target_pairs={{0,4},{2,6},{4,0},{6,2},{8,12},{10,14},{12,8},{14,10},{1,5},{3,7},... | collective-permute-start | bytes 393224 | tf_op jit(solution)/shard_map/ppermute | solution.py:276
  19.6 0.5 %collective-permute-start.5 = (bf16[64,1024]{1,0:T(8,128)(2,1)S(1)}, bf16[64,1024]{1,0:T(8,128)(2,1)S(1)}, u32[]{:S(2)}, u32[]{:S(2)}) collective-permute-start(bf16[64,1024]{1,0:T(8,128)(2,1)S(1)} %get-tuple-element.38), channel_id=1, source_target_pairs={{0,2},{2,0},{4,6},{6,4},{8,10},{10,8},{12,14},{14,12},{1,3},{3,1},... | collective-permute-start | bytes 393224 | tf_op jit(solution)/shard_map/ppermute | solution.py:276
  20.2 1.7 %collective-permute-done.7.far_ref = bf16[64,1024]{1,0:T(8,128)(2,1)S(1)} collective-permute-done((bf16[64,1024]{1,0:T(8,128)(2,1)S(1)}, bf16[64,1024]{1,0:T(8,128)(2,1)S(1)}, u32[]{:S(2)}, u32[]{:S(2)}) %collective-permute-start.7) | collective-permute-done | bytes 131104 | tf_op jit(solution)/shard_map/ppermute | solution.py:276
  21.9 0.1 collective-permute-start.8
  22.0 2.3 %collective-permute-done.3.refs_1_ = bf16[64,1024]{1,0:T(8,128)(2,1)S(1)} collective-permute-done((bf16[64,1024]{1,0:T(8,128)(2,1)S(1)}, bf16[64,1024]{1,0:T(8,128)(2,1)S(1)}, u32[]{:S(2)}, u32[]{:S(2)}) %collective-permute-start.3) | collective-permute-done | bytes 131104 | tf_op jit(solution)/shard_map/ppermute | solution.py:276
  24.3 1.9 %collective-permute-done.4.refs_2_ = bf16[64,1024]{1,0:T(8,128)(2,1)S(1)} collective-permute-done((bf16[64,1024]{1,0:T(8,128)(2,1)S(1)}, bf16[64,1024]{1,0:T(8,128)(2,1)S(1)}, u32[]{:S(2)}, u32[]{:S(2)}) %collective-permute-start.4) | collective-permute-done | bytes 131104 | tf_op jit(solution)/shard_map/ppermute | solution.py:276
  26.1 0.2 shard_map.57
  26.4 0.3 collective-permute-start.6
  26.6 0.1 copy.8.table_ref
  26.7 8.1 %shard_map.60.refs_0_ = bf16[8,18,2,256,256]{4,3,2,1,0:T(8,128)(2,1)} custom-call(s32[18,2]{1,0:T(8,128)S(1)} %copy.8.table_ref, bf16[64,1024]{1,0:T(8,128)(2,1)S(1)} %shard_map.59.own_ref, bf16[64,1024]{1,0:T(8,128)(2,1)S(1)} %collective-permute-done.8.other_ref), custom_call_target="tpu_custom_call" | custom-call | flops 268435456 | bytes 1048576 | tf_op jit(solution)/shard_map/pallas_call | solution.py:226
  34.9 0.1 collective-permute-start.9
  35.0 1.3 %collective-permute-done.9.other_ref = bf16[64,1024]{1,0:T(8,128)(2,1)S(1)} collective-permute-done((bf16[64,1024]{1,0:T(8,128)(2,1)S(1)}, bf16[64,1024]{1,0:T(8,128)(2,1)S(1)}, u32[]{:S(2)}, u32[]{:S(2)}) %collective-permute-start.9) | collective-permute-done | bytes 131104 | tf_op jit(solution)/shard_map/ppermute | solution.py:244
  36.3 8.1 %shard_map.62 = bf16[8,18,2,256,256]{4,3,2,1,0:T(8,128)(2,1)} custom-call(s32[18,2]{1,0:T(8,128)S(1)} %copy.8.table_ref, bf16[64,1024]{1,0:T(8,128)(2,1)S(1)} %shard_map.61.own_ref, bf16[64,1024]{1,0:T(8,128)(2,1)S(1)} %collective-permute-done.9.other_ref, bf16[8,18,2,256,256]{4,3,2,1,0:T(8,128)(2,1)} %shard_map.60.refs_0_), custom_call_target="tpu_custom_call", output_to_operand_aliasing={{}: (3, {})} | custom-call | flops 268435456 | bytes 1048576 | tf_op jit(solution)/shard_map/pallas_call | solution.py:226
  (7 shorter events, 0.1 us)
Async XLA Ops:
  3.0 23.6 %copy-start = (s32[18,2]{0,1:T(2,128)S(1)}, s32[18,2]{0,1:T(2,128)}, u32[]{:S(2)}) copy-start(s32[18,2]{0,1:T(2,128)} %param.7) | copy-start | bytes 436
  3.0 8.8 %collective-permute-start = (bf16[64,1024]{1,0:T(8,128)(2,1)S(1)}, bf16[64,1024]{1,0:T(8,128)(2,1)S(1)}, u32[]{:S(2)}, u32[]{:S(2)}) collective-permute-start(bf16[64,1024]{1,0:T(8,128)(2,1)S(1)} %get-tuple-element.28), channel_id=1, source_target_pairs={{0,2},{2,0},{4,6},{6,4},{8,10},{10,8},{12,14},{14,12},{1,3},{3,1},... | collective-permute-start | bytes 393224 | tf_op jit(solution)/shard_map/ppermute | solution.py:276
  6.1 6.4 %collective-permute-start.1 = (bf16[64,1024]{1,0:T(8,128)(2,1)S(1)}, bf16[64,1024]{1,0:T(8,128)(2,1)S(1)}, u32[]{:S(2)}, u32[]{:S(2)}) collective-permute-start(bf16[64,1024]{1,0:T(8,128)(2,1)S(1)} %get-tuple-element.29), channel_id=1, source_target_pairs={{0,4},{2,6},{4,0},{6,2},{8,12},{10,14},{12,8},{14,10},{1,5},{3,7},... | collective-permute-start | bytes 393224 | tf_op jit(solution)/shard_map/ppermute | solution.py:276
  7.6 6.0 %collective-permute-start.2 = (bf16[64,1024]{1,0:T(8,128)(2,1)S(1)}, bf16[64,1024]{1,0:T(8,128)(2,1)S(1)}, u32[]{:S(2)}, u32[]{:S(2)}) collective-permute-start(bf16[64,1024]{1,0:T(8,128)(2,1)S(1)} %get-tuple-element.30), channel_id=1, source_target_pairs={{0,6},{2,4},{4,2},{6,0},{8,14},{10,12},{12,10},{14,8},{1,7},{3,5},... | collective-permute-start | bytes 393224 | tf_op jit(solution)/shard_map/ppermute | solution.py:276
  13.8 8.0 %collective-permute-start.7 = (bf16[64,1024]{1,0:T(8,128)(2,1)S(1)}, bf16[64,1024]{1,0:T(8,128)(2,1)S(1)}, u32[]{:S(2)}, u32[]{:S(2)}) collective-permute-start(bf16[64,1024]{1,0:T(8,128)(2,1)S(1)} %get-tuple-element.46), channel_id=1, source_target_pairs={{0,8},{2,10},{4,12},{6,14},{8,0},{10,2},{12,4},{14,6},{1,9},{3,11}... | collective-permute-start | bytes 393224 | tf_op jit(solution)/shard_map/ppermute | solution.py:276
  16.7 7.6 %collective-permute-start.3 = (bf16[64,1024]{1,0:T(8,128)(2,1)S(1)}, bf16[64,1024]{1,0:T(8,128)(2,1)S(1)}, u32[]{:S(2)}, u32[]{:S(2)}) collective-permute-start(bf16[64,1024]{1,0:T(8,128)(2,1)S(1)} %get-tuple-element.36), channel_id=1, source_target_pairs={{0,6},{2,4},{4,2},{6,0},{8,14},{10,12},{12,10},{14,8},{1,7},{3,5},... | collective-permute-start | bytes 393224 | tf_op jit(solution)/shard_map/ppermute | solution.py:276
  19.2 7.0 %collective-permute-start.4 = (bf16[64,1024]{1,0:T(8,128)(2,1)S(1)}, bf16[64,1024]{1,0:T(8,128)(2,1)S(1)}, u32[]{:S(2)}, u32[]{:S(2)}) collective-permute-start(bf16[64,1024]{1,0:T(8,128)(2,1)S(1)} %get-tuple-element.37), channel_id=1, source_target_pairs={{0,4},{2,6},{4,0},{6,2},{8,12},{10,14},{12,8},{14,10},{1,5},{3,7},... | collective-permute-start | bytes 393224 | tf_op jit(solution)/shard_map/ppermute | solution.py:276
  19.6 6.5 %collective-permute-start.5 = (bf16[64,1024]{1,0:T(8,128)(2,1)S(1)}, bf16[64,1024]{1,0:T(8,128)(2,1)S(1)}, u32[]{:S(2)}, u32[]{:S(2)}) collective-permute-start(bf16[64,1024]{1,0:T(8,128)(2,1)S(1)} %get-tuple-element.38), channel_id=1, source_target_pairs={{0,2},{2,0},{4,6},{6,4},{8,10},{10,8},{12,14},{14,12},{1,3},{3,1},... | collective-permute-start | bytes 393224 | tf_op jit(solution)/shard_map/ppermute | solution.py:276
  21.9 4.8 %collective-permute-start.8 = (bf16[64,1024]{1,0:T(8,128)(2,1)S(1)}, bf16[64,1024]{1,0:T(8,128)(2,1)S(1)}, u32[]{:S(2)}, u32[]{:S(2)}) collective-permute-start(bf16[64,1024]{1,0:T(8,128)(2,1)S(1)} %shard_map.59.own_ref), channel_id=1, source_target_pairs={{0,1},{1,0},{2,3},{3,2},{4,5},{5,4},{6,7},{7,6},{8,9},{9,8},{10,11... | collective-permute-start | bytes 393224 | tf_op jit(solution)/shard_map/ppermute | solution.py:244
  26.4 8.5 %collective-permute-start.6 = (bf16[64,1024]{1,0:T(8,128)(2,1)S(1)}, bf16[64,1024]{1,0:T(8,128)(2,1)S(1)}, u32[]{:S(2)}, u32[]{:S(2)}) collective-permute-start(bf16[64,1024]{1,0:T(8,128)(2,1)S(1)} %get-tuple-element.40), channel_id=1, source_target_pairs={{0,8},{2,10},{4,12},{6,14},{8,0},{10,2},{12,4},{14,6},{1,9},{3,11}... | collective-permute-start | bytes 393224 | tf_op jit(solution)/shard_map/ppermute | solution.py:276
  34.9 1.4 %collective-permute-start.9 = (bf16[64,1024]{1,0:T(8,128)(2,1)S(1)}, bf16[64,1024]{1,0:T(8,128)(2,1)S(1)}, u32[]{:S(2)}, u32[]{:S(2)}) collective-permute-start(bf16[64,1024]{1,0:T(8,128)(2,1)S(1)} %shard_map.61.own_ref), channel_id=1, source_target_pairs={{0,1},{1,0},{2,3},{3,2},{4,5},{5,4},{6,7},{7,6},{8,9},{9,8},{10,11... | collective-permute-start | bytes 393224 | tf_op jit(solution)/shard_map/ppermute | solution.py:244
